TPU v7x, 32 devices: a whole 2x2x4 slice. The times are simulated.
32 devices in a mesh: seg: 4 (over z), tm: 8 (over y, x, core).
Axes of the slice: x: 2, y: 2, z: 4, core: 2. Of those that a mesh axis runs over, the one named last changes fastest.
Arguments:
- feats: bfloat16 [32, 4096, 192], P('seg', 'tm'), may hold values from -6 to 6
- spectral: bfloat16 [32, 1024, 384], P('seg', 'tm'), may hold values from -6 to 6
- target: bfloat16 [32, 1024, 128], P('seg', 'tm'), may hold values from -6 to 6
- valid_samples: int32 [32], P('seg'), may hold values from 5461 to 16384, as said below
- stem_weights: int32 [32, 4], P('seg'), may hold values from 1 to 4
- conv_weight: float32 [1536, 384], P('tm'), may hold values from -0.15625 to 0.15625
- query_weight: float32 [384, 384], P('tm'), may hold values from -0.046875 to 0.046875
- keyval_weight: float32 [384, 768], P('tm'), may hold values from -0.3125 to 0.3125
- out_weight: float32 [384, 384], P('tm'), may hold values from -6 to 6
- up_weight: float32 [384, 1536], P('tm'), may hold values from -0.3125 to 0.3125
- down_weight: float32 [1536, 384], P('tm'), may hold values from -0.15625 to 0.15625
- head_weight: float32 [384, 128], P('tm'), may hold values from -0.3125 to 0.3125
- gains: float32 [5, 384], P(None, 'tm'), may hold values from 0.5 to 1.5
- conv_first: float32 [1536, 384], P('tm'), as said below
- query_first: float32 [384, 384], P('tm')
- keyval_first: float32 [384, 768], P('tm')
- out_first: float32 [384, 384], P('tm')
- up_first: float32 [384, 1536], P('tm')
- down_first: float32 [1536, 384], P('tm')
- head_first: float32 [384, 128], P('tm')
- gain_first: float32 [5, 384], P(None, 'tm')
- conv_second: float32 [1536, 384], P('tm'), as said below
- query_second: float32 [384, 384], P('tm')
- keyval_second: float32 [384, 768], P('tm')
- out_second: float32 [384, 384], P('tm')
- up_second: float32 [384, 1536], P('tm')
- down_second: float32 [1536, 384], P('tm')
- head_second: float32 [384, 128], P('tm')
- gain_second: float32 [5, 384], P(None, 'tm')
Outputs:
- loss_sum: float32 [], replicated
- sample_count: float32 [], replicated
- grad_norm: float32 [], replicated
- conv_new: float32 [1536, 384], P('tm')
- query_new: float32 [384, 384], P('tm')
- keyval_new: float32 [384, 768], P('tm')
- out_new: float32 [384, 384], P('tm')
- up_new: float32 [384, 1536], P('tm')
- down_new: float32 [1536, 384], P('tm')
- head_new: float32 [384, 128], P('tm')
- gains_new: float32 [5, 384], P(None, 'tm')
- conv_first_new: float32 [1536, 384], P('tm')
- query_first_new: float32 [384, 384], P('tm')
- keyval_first_new: float32 [384, 768], P('tm')
- out_first_new: float32 [384, 384], P('tm')
- up_first_new: float32 [384, 1536], P('tm')
- down_first_new: float32 [1536, 384], P('tm')
- head_first_new: float32 [384, 128], P('tm')
- gain_first_new: float32 [5, 384], P(None, 'tm')
- conv_second_new: float32 [1536, 384], P('tm')
- query_second_new: float32 [384, 384], P('tm')
- keyval_second_new: float32 [384, 768], P('tm')
- out_second_new: float32 [384, 384], P('tm')
- up_second_new: float32 [384, 1536], P('tm')
- down_second_new: float32 [1536, 384], P('tm')
- head_second_new: float32 [384, 128], P('tm')
- gain_second_new: float32 [5, 384], P(None, 'tm')
Inputs may be any that keep to these rules, and one draw needn't show every extreme that they name: `valid_samples`: in each aligned run of 8 segments (those of one index of seg) at least one segment has more than 14336 valid samples; some segment is complete. `conv_first`: first moments have both signs. `conv_second`: second moments are positive.
All inputs are finite; a program needn't handle non-finite values.
Results may differ from a plain program's by a relative error of at most 0.005.
The roundings to bfloat16 on the way count: a program that leaves them out, or rounds other values in their place, can miss the bound.
Values may be sent and summed in bfloat16 or wider, within the bound.
No kernel may reach another device: no remote copies, remote signals or barrier semaphores. Data moves between devices by JAX's collectives and lax.ppermute only.
A program may use at most 320 MiB of HBM per device.

v0:
```python
import jax
import jax.numpy as jnp
from jax import lax
from jax.sharding import PartitionSpec as P

H = 8
STEMS = 4
SUB = 16
STEP = 10


clip_limit = 0.001
beta_first = 0.9
beta_second = 0.999
learn_rate = 0.03
fast_rate = 0.5
weight_decay = 0.05
adam_epsilon = 1e-08
norm_epsilon = 1e-05


def with_halo(cells, sides, width):
    for axis, dim in sides:
        count = lax.axis_size(axis)
        ends = count - 1
        head = lax.slice_in_dim(cells, 0, width, axis=dim)
        tail = lax.slice_in_dim(cells, cells.shape[dim] - width, cells.shape[dim], axis=dim)
        cells = jnp.concatenate(
            [
                lax.ppermute(tail, axis, [(i, (i + 1) % count) for i in range(ends)]),
                cells,
                lax.ppermute(head, axis, [((i + 1) % count, i) for i in range(ends)]),
            ],
            axis=dim,
        )
    return cells


def layer_norm(values, gain):
    centred = values - jnp.mean(values, -1, keepdims=True)
    return centred * lax.rsqrt(jnp.mean(centred * centred, -1, keepdims=True) + norm_epsilon) * gain


def gelu_exact(values):
    return jax.nn.gelu(values, approximate=False)


def norm_back(values, gain, upstream):
    result, pullback = jax.vjp(layer_norm, values, gain)
    value_grad, gain_grad = pullback(upstream)
    return (value_grad, gain_grad)


def gelu_back(values, upstream):
    result, pullback = jax.vjp(gelu_exact, values)
    return pullback(upstream)[0]


def outer_sum(left, right):
    return lax.dot_general(
        left, right, (((0,), (0,)), ((), ())), preferred_element_type=jnp.float32
    )


def back_product(upstream, weight):
    return lax.dot_general(
        upstream, weight, (((1,), (1,)), ((), ())), preferred_element_type=jnp.float32
    )


def project_rows(normed_all, weight):
    segments, length, width = normed_all.shape
    joined = jnp.dot(
        normed_all.reshape(segments * length, width), weight, preferred_element_type=jnp.float32
    )
    return joined.astype(jnp.bfloat16).reshape(segments, length, weight.shape[1])


def split_block(keys_all, offset, block_size, head_count):
    block = lax.dynamic_slice_in_dim(keys_all, offset, block_size, 1)
    segments, length, doubled = block.shape
    half_width = doubled // 2
    keys_block = block[..., :half_width].reshape(
        segments, length, head_count, half_width // head_count
    )
    values_block = block[..., half_width:].reshape(
        segments, length, head_count, half_width // head_count
    )
    return (keys_block, values_block)


def block_scores(queries, keys_block):
    return jnp.einsum("sqhd,skhd->sqhk", queries, keys_block, preferred_element_type=jnp.float32)


def block_layout(queries, keys_all):
    key_total = keys_all.shape[1]
    block_size = min(256, key_total)
    return (block_size, key_total // block_size, queries.shape[2])


def softmax_totals(queries, keys_all):
    block_size, blocks, head_count = block_layout(queries, keys_all)

    def advance(position, carry):
        running_max, mass_sum = carry
        keys_block, values_block = split_block(
            keys_all, position * block_size, block_size, head_count
        )
        scores = block_scores(queries, keys_block)
        new_max = jnp.maximum(running_max, jnp.max(scores, -1))
        mass_sum = mass_sum * jnp.exp(running_max - new_max) + jnp.sum(
            jnp.exp(scores - new_max[..., None]), -1
        )
        return (new_max, mass_sum)

    start_max = jnp.full(queries.shape[:3], -1e30, jnp.float32)
    running_max, mass_sum = lax.fori_loop(
        0, blocks, advance, (start_max, jnp.zeros(queries.shape[:3], jnp.float32))
    )
    return running_max + jnp.log(mass_sum)


def attend(queries, keys_all, totals):
    block_size, blocks, head_count = block_layout(queries, keys_all)

    def add_block(position, running):
        keys_block, values_block = split_block(
            keys_all, position * block_size, block_size, head_count
        )
        probs = jnp.exp(block_scores(queries, keys_block) - totals[..., None]).astype(jnp.bfloat16)
        return running + jnp.einsum(
            "sqhk,skhd->sqhd", probs, values_block, preferred_element_type=jnp.float32
        )

    return lax.fori_loop(0, blocks, add_block, jnp.zeros(queries.shape, jnp.float32))


def attend_back(queries, keys_all, totals, upstream):
    block_size, blocks, head_count = block_layout(queries, keys_all)
    segments = queries.shape[0]

    def block_terms(position):
        keys_block, values_block = split_block(
            keys_all, position * block_size, block_size, head_count
        )
        probs = jnp.exp(block_scores(queries, keys_block) - totals[..., None])
        pressure = jnp.einsum(
            "sqhd,skhd->sqhk", upstream, values_block, preferred_element_type=jnp.float32
        )
        return (keys_block, probs, pressure)

    def delta_step(position, running):
        keys_block, probs, pressure = block_terms(position)
        return running + jnp.sum(probs * pressure, -1)

    delta = lax.fori_loop(0, blocks, delta_step, jnp.zeros(totals.shape, jnp.float32))

    def grad_step(position, carry):
        query_grad, keyval_grad = carry
        keys_block, probs, pressure = block_terms(position)
        score_grad = (probs * (pressure - delta[..., None])).astype(jnp.bfloat16)
        query_grad = query_grad + jnp.einsum(
            "sqhk,skhd->sqhd", score_grad, keys_block, preferred_element_type=jnp.float32
        )
        key_grad = jnp.einsum(
            "sqhk,sqhd->skhd", score_grad, queries, preferred_element_type=jnp.float32
        )
        value_grad = jnp.einsum(
            "sqhk,sqhd->skhd",
            probs.astype(jnp.bfloat16),
            upstream,
            preferred_element_type=jnp.float32,
        )
        joined = jnp.concatenate(
            [
                key_grad.reshape(segments, block_size, -1),
                value_grad.reshape(segments, block_size, -1),
            ],
            -1,
        )
        keyval_grad = lax.dynamic_update_slice_in_dim(keyval_grad, joined, position * block_size, 1)
        return (query_grad, keyval_grad)

    start = (jnp.zeros(queries.shape, jnp.float32), jnp.zeros(keys_all.shape, jnp.float32))
    return lax.fori_loop(0, blocks, grad_step, start)


def adam_update(master, first, second, grad, factor, rate):
    clipped = grad * factor
    first_new = beta_first * first + (1.0 - beta_first) * clipped
    second_new = beta_second * second + (1.0 - beta_second) * clipped * clipped
    moment_hat = first_new / (1.0 - beta_first**STEP)
    square_hat = second_new / (1.0 - beta_second**STEP)
    master_new = master - rate * (
        moment_hat / (jnp.sqrt(square_hat) + adam_epsilon) + weight_decay * master
    )
    return (master_new, first_new, second_new)


def on_device(
    feats,
    spectral,
    target,
    valid_samples,
    stem_weights,
    conv_weight,
    query_weight,
    keyval_weight,
    out_weight,
    up_weight,
    down_weight,
    head_weight,
    gains,
    conv_first,
    query_first,
    keyval_first,
    out_first,
    up_first,
    down_first,
    head_first,
    gain_first,
    conv_second,
    query_second,
    keyval_second,
    out_second,
    up_second,
    down_second,
    head_second,
    gain_second,
):
    bfloat = jnp.bfloat16
    (
        whole_conv,
        whole_query,
        whole_keyval,
        whole_out,
        whole_up,
        whole_down,
        whole_head,
        whole_gains,
    ) = (
        lax.all_gather(conv_weight.astype(bfloat), "tm", axis=0, tiled=True),
        lax.all_gather(query_weight.astype(bfloat), "tm", axis=0, tiled=True),
        lax.all_gather(keyval_weight.astype(bfloat), "tm", axis=0, tiled=True),
        lax.all_gather(out_weight.astype(bfloat), "tm", axis=0, tiled=True),
        lax.all_gather(up_weight.astype(bfloat), "tm", axis=0, tiled=True),
        lax.all_gather(down_weight.astype(bfloat), "tm", axis=0, tiled=True),
        lax.all_gather(head_weight.astype(bfloat), "tm", axis=0, tiled=True),
        lax.all_gather(gains.astype(bfloat), "tm", axis=1, tiled=True),
    )
    gain_rows = whole_gains.astype(jnp.float32)
    segments, frame_count, channels = feats.shape
    queries_dev = frame_count // 4
    row_count = segments * queries_dev
    model_width = whole_query.shape[1]
    head_count = H
    head_size = model_width // head_count
    spectral_dev = spectral.shape[1]
    out_width = target.shape[2]
    padded = with_halo(feats, (("tm", 1),), 2)
    front = padded[:, :frame_count].reshape(segments, queries_dev, 4 * channels)
    behind = padded[:, 4 : frame_count + 4].reshape(segments, queries_dev, 4 * channels)
    unfolded = jnp.concatenate([front, behind], -1).reshape(row_count, 8 * channels)
    conv_out = jnp.dot(unfolded, whole_conv, preferred_element_type=jnp.float32)
    stream = gelu_exact(conv_out)
    normed = layer_norm(stream, gain_rows[0]).astype(bfloat)
    queries = jnp.dot(normed, whole_query, preferred_element_type=jnp.float32).astype(bfloat)
    queries = queries.reshape(segments, queries_dev, head_count, head_size)
    spectral_rows = spectral.reshape(segments * spectral_dev, model_width).astype(jnp.float32)
    spectral_normed = layer_norm(spectral_rows, gain_rows[1]).astype(bfloat)
    normed_local = spectral_normed.reshape(segments, spectral_dev, model_width)
    keyval = project_rows(normed_local, whole_keyval)
    keys_all = lax.all_gather(keyval, "tm", axis=1, tiled=True)
    totals = softmax_totals(queries, keys_all)
    attended = attend(queries, keys_all, totals).reshape(row_count, model_width).astype(bfloat)
    branch = jnp.dot(attended, whole_out, preferred_element_type=jnp.float32)
    stream_mid = stream + gain_rows[3] * branch
    ffn_in = layer_norm(stream_mid, gain_rows[2]).astype(bfloat)
    hidden = jnp.dot(ffn_in, whole_up, preferred_element_type=jnp.float32)
    activated = gelu_exact(hidden).astype(bfloat)
    ffn_out = jnp.dot(activated, whole_down, preferred_element_type=jnp.float32)
    stream_end = stream_mid + gain_rows[4] * ffn_out
    stream_low = stream_end.astype(bfloat)
    predicted = jnp.dot(stream_low, whole_head, preferred_element_type=jnp.float32).reshape(
        segments, queries_dev, out_width
    )
    tm_place = lax.axis_index("tm")
    columns = jnp.arange(out_width)
    position = (tm_place * queries_dev + jnp.arange(queries_dev))[:, None] * SUB + (columns % SUB)[
        None, :
    ]
    live = (position[None] < valid_samples[:, None, None]).astype(jnp.float32)
    chosen = ((columns // (2 * SUB))[:, None] == jnp.arange(STEMS)[None, :]).astype(jnp.float32)
    per_column = jnp.sum(stem_weights.astype(jnp.float32)[:, None, :] * chosen[None], -1)
    mask_weights = live * per_column[:, None, :]
    error = predicted - target.astype(jnp.float32)
    loss_part = jnp.sum(mask_weights * (jnp.sqrt(error * error + 1.0) - 1.0))
    count_part = jnp.sum(
        jnp.clip(valid_samples - tm_place * queries_dev * SUB, 0, queries_dev * SUB)
    ).astype(jnp.float32)
    loss_sum, sample_count = lax.psum((loss_part, count_part), ("seg", "tm"))
    predicted_grad = (mask_weights * error / jnp.sqrt(error * error + 1.0) / sample_count).astype(
        bfloat
    )
    predicted_grad = predicted_grad.reshape(row_count, out_width)
    grad_head = outer_sum(stream_low, predicted_grad)
    stream_end_grad = back_product(predicted_grad, whole_head)
    ffn_grad = (gain_rows[4] * stream_end_grad).astype(bfloat)
    grad_scale_ffn = jnp.sum(stream_end_grad * ffn_out, 0)
    grad_down = outer_sum(activated, ffn_grad)
    activated_grad = back_product(ffn_grad, whole_down)
    hidden_grad = gelu_back(hidden, activated_grad).astype(bfloat)
    grad_up = outer_sum(ffn_in, hidden_grad)
    ffn_in_grad = back_product(hidden_grad, whole_up)
    mid_part, grad_gain_ffn = norm_back(stream_mid, gain_rows[2], ffn_in_grad)
    stream_mid_grad = stream_end_grad + mid_part
    branch_grad = (gain_rows[3] * stream_mid_grad).astype(bfloat)
    grad_scale_attn = jnp.sum(stream_mid_grad * branch, 0)
    grad_out = outer_sum(attended, branch_grad)
    attended_grad = (
        back_product(branch_grad, whole_out)
        .astype(bfloat)
        .reshape(segments, queries_dev, head_count, head_size)
    )
    keys_back = lax.all_gather(project_rows(normed_local, whole_keyval), "tm", axis=1, tiled=True)
    query_grad, keyval_grad_all = attend_back(queries, keys_back, totals, attended_grad)
    keyval_grad = lax.psum_scatter(keyval_grad_all, "tm", scatter_dimension=1, tiled=True)
    keyval_grad = keyval_grad.astype(bfloat).reshape(segments * spectral_dev, 2 * model_width)
    query_grad = query_grad.reshape(row_count, model_width).astype(bfloat)
    grad_query = outer_sum(normed, query_grad)
    normed_grad = back_product(query_grad, whole_query)
    stream_part, grad_gain_query = norm_back(stream, gain_rows[0], normed_grad)
    stream_grad = stream_mid_grad + stream_part
    conv_grad = gelu_back(conv_out, stream_grad).astype(bfloat)
    grad_conv = outer_sum(unfolded, conv_grad)
    grad_keyval = outer_sum(spectral_normed, keyval_grad)
    spectral_grad = back_product(keyval_grad, whole_keyval)
    unused_grad, grad_gain_keys = norm_back(spectral_rows, gain_rows[1], spectral_grad)
    grad_gains = jnp.stack(
        [grad_gain_query, grad_gain_keys, grad_gain_ffn, grad_scale_attn, grad_scale_ffn]
    )
    shards = (
        lax.psum_scatter(grad_conv, "tm", scatter_dimension=0, tiled=True),
        lax.psum_scatter(grad_query, "tm", scatter_dimension=0, tiled=True),
        lax.psum_scatter(grad_keyval, "tm", scatter_dimension=0, tiled=True),
        lax.psum_scatter(grad_out, "tm", scatter_dimension=0, tiled=True),
        lax.psum_scatter(grad_up, "tm", scatter_dimension=0, tiled=True),
        lax.psum_scatter(grad_down, "tm", scatter_dimension=0, tiled=True),
        lax.psum_scatter(grad_head, "tm", scatter_dimension=0, tiled=True),
        lax.psum_scatter(grad_gains, "tm", scatter_dimension=1, tiled=True),
    )
    reduced = lax.psum(
        (shards[0], shards[1], shards[2], shards[3], shards[4], shards[5], shards[6], shards[7]),
        "seg",
    )
    local_squares = jnp.zeros((), jnp.float32)
    for shard in reduced:
        local_squares = local_squares + jnp.sum(shard * shard)
    squares = lax.psum(local_squares, "tm")
    grad_norm = jnp.sqrt(squares)
    factor = jnp.minimum(1.0, clip_limit / (grad_norm + 1e-06))
    masters = (
        conv_weight,
        query_weight,
        keyval_weight,
        out_weight,
        up_weight,
        down_weight,
        head_weight,
        gains,
    )
    firsts = (
        conv_first,
        query_first,
        keyval_first,
        out_first,
        up_first,
        down_first,
        head_first,
        gain_first,
    )
    seconds = (
        conv_second,
        query_second,
        keyval_second,
        out_second,
        up_second,
        down_second,
        head_second,
        gain_second,
    )
    rates = (
        learn_rate,
        learn_rate,
        learn_rate,
        fast_rate,
        learn_rate,
        learn_rate,
        learn_rate,
        fast_rate,
    )
    updated = [
        adam_update(m, f, s, g, factor, r)
        for m, f, s, g, r in zip(masters, firsts, seconds, reduced, rates)
    ]
    return (
        loss_sum,
        sample_count,
        grad_norm,
        updated[0][0],
        updated[1][0],
        updated[2][0],
        updated[3][0],
        updated[4][0],
        updated[5][0],
        updated[6][0],
        updated[7][0],
        updated[0][1],
        updated[1][1],
        updated[2][1],
        updated[3][1],
        updated[4][1],
        updated[5][1],
        updated[6][1],
        updated[7][1],
        updated[0][2],
        updated[1][2],
        updated[2][2],
        updated[3][2],
        updated[4][2],
        updated[5][2],
        updated[6][2],
        updated[7][2],
    )


def solution(mesh):
    return jax.shard_map(
        on_device,
        mesh=mesh,
        in_specs=(
            P("seg", "tm", None),
            P("seg", "tm", None),
            P("seg", "tm", None),
            P("seg"),
            P("seg", None),
            P("tm", None),
            P("tm", None),
            P("tm", None),
            P("tm", None),
            P("tm", None),
            P("tm", None),
            P("tm", None),
            P(None, "tm"),
            P("tm", None),
            P("tm", None),
            P("tm", None),
            P("tm", None),
            P("tm", None),
            P("tm", None),
            P("tm", None),
            P(None, "tm"),
            P("tm", None),
            P("tm", None),
            P("tm", None),
            P("tm", None),
            P("tm", None),
            P("tm", None),
            P("tm", None),
            P(None, "tm"),
        ),
        out_specs=(
            P(),
            P(),
            P(),
            P("tm", None),
            P("tm", None),
            P("tm", None),
            P("tm", None),
            P("tm", None),
            P("tm", None),
            P("tm", None),
            P(None, "tm"),
            P("tm", None),
            P("tm", None),
            P("tm", None),
            P("tm", None),
            P("tm", None),
            P("tm", None),
            P("tm", None),
            P(None, "tm"),
            P("tm", None),
            P("tm", None),
            P("tm", None),
            P("tm", None),
            P("tm", None),
            P("tm", None),
            P("tm", None),
            P(None, "tm"),
        ),
        check_vma=False,
    )
```

profile of v0, /device:TPU:0, one launch (start us, length us, event | category | flops | bytes accessed | tf_op | source)
XLA Modules:
  0.0 1004.5 jit_solution(11917573246651883375)
XLA Ops:
  9.7 10.3 %all-gather = bf16[8,48,5]{1,2,0:T(8,128)(2,1)S(1)} all-gather(bf16[1,48,5]{1,2,0:T(8,128)(2,1)S(1)} %convert_bitcast_fusion), channel_id=1, replica_groups=mesh['seg'=4,'tm'=8] {'tm'}, dimensions={0}, use_global_device_ids=true | all-gather | bytes 4320 | tf_op jit(solution)/shard_map/all_gather | solution.py:250
  21.7 10.0 all_gather.30
  39.7 3.8 collective-permute-start
  44.4 15.9 %all_gather.33 = bf16[384,384]{1,0:T(8,128)(2,1)S(1)} all-gather(bf16[48,384]{1,0:T(8,128)(2,1)S(1)} %convert_element_type.150), channel_id=1, replica_groups=mesh['seg'=4,'tm'=8] {'tm'}, dimensions={0}, use_global_device_ids=true | all-gather | bytes 331776 | tf_op jit(solution)/shard_map/all_gather | solution.py:246
  60.2 12.2 %all_gather.32 = bf16[384,384]{1,0:T(8,128)(2,1)S(1)} all-gather(bf16[48,384]{1,0:T(8,128)(2,1)S(1)} %convert_element_type.146), channel_id=1, replica_groups=mesh['seg'=4,'tm'=8] {'tm'}, dimensions={0}, use_global_device_ids=true | all-gather | bytes 331776 | tf_op jit(solution)/shard_map/all_gather | solution.py:244
  73.3 9.5 all_gather.36
  83.4 4.8 pad_maximum_fusion.1
  88.2 2.7 copy.154
  90.9 3.0 concatenate.25
  93.9 2.7 copy.153
  96.7 3.0 concatenate.23
  99.7 2.8 constant_dynamic-update-slice_fusion.2
  103.9 7.8 fusion.92
  114.3 3.7 all-gather.8.cloned.1.call-done
  118.1 21.9 %while.60 = (s32[]{:T(128)}, f32[8,128,8]{1,2,0:T(8,128)S(1)}, f32[8,128,8]{1,2,0:T(8,128)S(1)}, bf16[8,1024,768]{1,2,0:T(8,128)(2,1)}, bf16[8,128,8,48]{1,3,2,0...) while((s32[]{:T(128)}, f32[8,128,8]{1,2,0:T(8,128)S(1)}, ...), condition=%wide.region_8.0_spmd.clone, body=%wide.region_5.8_spmd.clone.sunk | while | flops 207659008 | bytes 22708384 | solution.py:118
  121.3 2.4 fusion.173
  140.0 34.2 %while.61 = (s32[]{:T(128)}, f32[8,128,8,48]{1,3,2,0:T(8,128)}, bf16[8,1024,768]{1,2,0:T(8,128)(2,1)}, bf16[8,128,8,48]{1,3,2,0:T(8,128)(2,1)S(1)}, f32[8,128,8]...) while((s32[]{:T(128)}, f32[8,128,8,48]{1,3,2,0:T(8,128)}, ...), condition=%wide.region_10.0_spmd.clone, body=%wide.region_9.0_spmd.clone.sunk | while | flops 407633920 | bytes 13402297 | solution.py:136
  140.0 3.3 constant_dynamic-slice_fusion.12
  143.4 4.9 bitcast_add_fusion.4
  148.2 3.3 constant_dynamic-slice_fusion.12
  151.6 5.3 bitcast_add_fusion.4
  156.9 3.3 constant_dynamic-slice_fusion.12
  160.2 5.3 bitcast_add_fusion.4
  165.5 3.3 constant_dynamic-slice_fusion.12
  168.9 5.4 bitcast_add_fusion.4
  178.9 18.2 %multiply_convert_fusion = (bf16[1024,1536]{1,0:T(8,128)(2,1)}, f32[1024,1536]{1,0:T(8,128)}, f32[1024,1536]{1,0:T(8,128)}) fusion(bf16[384,1536]{1,0:T(8,128)(2,1)} %all-gather.10.cloned.1.call-done, f32[1024,384]{0,1:T(8,128)S(1)} %get-tuple-element.766, f32[384]{0:T(512)S(1)} %copy-done.76, f32[1024]{0:T(1024)S(1)} %fusion.70, ...), kind=kOutput, calls=%fused_computation.40 | convolution fusion | flops 1311768576 | bytes 18490880 | tf_op jit(solution)/shard_map/dot_general | solution.py:280
  197.1 5.1 fusion.97
  202.2 3.0 copy.161
  209.0 39.5 %all-reduce = (f32[]{:T(128)}, f32[]{:T(128)}) all-reduce(f32[]{:T(128)} %fusion.58, f32[]{:T(128)S(6)} %convert_element_type.158), channel_id=1, replica_groups=mesh['seg'=4,'tm'=8] {'seg','tm'}, use_global_device_ids=true, to_apply=%region_14.15 | all-reduce | flops 2 | bytes 16 | tf_op jit(solution)/shard_map/psum | solution.py:302
  250.4 3.6 multiply_reduce_fusion
  254.1 3.1 copy.164
  257.2 9.0 add_convert_fusion
  276.1 22.8 %while.62 = (s32[]{:T(128)}, f32[8,128,8]{1,2,0:T(8,128)S(1)}, bf16[8,1024,768]{1,2,0:T(8,128)(2,1)}, bf16[8,128,8,48]{1,3,2,0:T(8,128)(2,1)S(1)}, f32[8,128,8]{...) while((s32[]{:T(128)}, f32[8,128,8]{1,2,0:T(8,128)S(1)}, ...), condition=%wide.region_21.22_spmd.clone, body=%wide.region_19.21_spmd.clone.sunk | while | flops 408952832 | bytes 27951296 | solution.py:157
  298.9 10.5 %broadcast_in_dim.28.clone = f32[8,1024,768]{2,1,0:T(8,128)} broadcast(f32[]{:T(128)} %constant.330.clone.1), dimensions={} | broadcast | bytes 25165828 | tf_op jit(solution)/shard_map/broadcast_in_dim | solution.py:185
  309.4 103.5 %while.63 = (s32[]{:T(128)}, f32[8,128,8,48]{1,3,2,0:T(8,128)S(1)}, f32[8,1024,768]{2,1,0:T(8,128)}, bf16[8,1024,768]{1,2,0:T(8,128)(2,1)}, bf16[8,128,8,48]{1,3...) while((s32[]{:T(128)}, f32[8,128,8,48]{1,3,2,0:T(8,128)S(1)}, ...), condition=%wide.region_23.24_spmd.clone, body=%wide.region_22.23_spmd.clone.sunk | while | flops 1021575168 | bytes 99188944 | solution.py:186
  319.7 3.3 pad_maximum_fusion.4
  323.1 6.6 copy.235
  329.6 5.9 constant_dynamic-update-slice_fusion.4
  345.5 3.3 pad_maximum_fusion.4
  348.8 6.6 copy.235
  355.4 5.9 constant_dynamic-update-slice_fusion.4
  371.2 3.3 pad_maximum_fusion.4
  374.5 6.6 copy.235
  381.1 6.0 constant_dynamic-update-slice_fusion.4
  397.1 3.3 pad_maximum_fusion.4
  400.4 6.6 copy.235
  407.0 5.9 constant_dynamic-update-slice_fusion.4
  414.3 2.6 fusion.39
  420.4 5.4 fusion.77
  427.7 5.6 fusion.79
  438.4 9.1 fusion.34
  447.6 123.4 %reduce-scatter.16.cloned.1.call-done = f32[8,128,768]{2,1,0:T(8,128)} async-done(((f32[8,1024,768]{2,1,0:T(8,128)}), f32[8,128,768]{2,1,0:T(8,128)}) %reduce-scatter.16.cloned.1.call-update) | async-done | bytes 3145744 | tf_op jit(solution)/shard_map/reduce_scatter | solution.py:328
  576.5 2.5 multiply_reduce_fusion.3
  581.2 27.1 %reduce-scatter.20.cloned.1.call-done = f32[48,384]{1,0:T(8,128)} async-done(((f32[384,384]{1,0:T(8,128)}), f32[48,384]{1,0:T(8,128)}) %reduce-scatter.20.cloned.1.call-update) | async-done | bytes 73744 | tf_op jit(solution)/shard_map/reduce_scatter | solution.py:347
  608.3 37.5 %reduce-scatter.14.cloned.1.call-done = f32[48,384]{1,0:T(8,128)} async-done(((f32[384,384]{1,0:T(8,128)}), f32[48,384]{1,0:T(8,128)}) %reduce-scatter.14.cloned.1.call-update) | async-done | bytes 73744 | tf_op jit(solution)/shard_map/reduce_scatter | solution.py:345
  645.8 45.8 %reduce-scatter.24.cloned.1.call-done = f32[192,384]{1,0:T(8,128)} async-done(((f32[1536,384]{1,0:T(8,128)}), f32[192,384]{1,0:T(8,128)}) %reduce-scatter.24.cloned.1.call-update) | async-done | bytes 294928 | tf_op jit(solution)/shard_map/reduce_scatter | solution.py:349
  691.7 46.2 %reduce-scatter.22.cloned.1.call-done = f32[48,1536]{1,0:T(8,128)} async-done(((f32[384,1536]{1,0:T(8,128)}), f32[48,1536]{1,0:T(8,128)}) %reduce-scatter.22.cloned.1.call-update) | async-done | bytes 294928 | tf_op jit(solution)/shard_map/reduce_scatter | solution.py:348
  737.9 45.7 %reduce-scatter.12.cloned.1.call-done = f32[192,384]{1,0:T(8,128)} async-done(((f32[1536,384]{1,0:T(8,128)}), f32[192,384]{1,0:T(8,128)}) %reduce-scatter.12.cloned.1.call-update) | async-done | bytes 294928 | tf_op jit(solution)/shard_map/reduce_scatter | solution.py:344
  783.6 40.4 %reduce-scatter.18.cloned.1.call-done = f32[48,768]{1,0:T(8,128)} async-done(((f32[384,768]{1,0:T(8,128)}), f32[48,768]{1,0:T(8,128)}) %reduce-scatter.18.cloned.1.call-update) | async-done | bytes 147472 | tf_op jit(solution)/shard_map/reduce_scatter | solution.py:346
  824.0 36.9 %reduce-scatter.28.cloned.1.call-done = f32[48,5]{1,0:T(8,128)} async-done(((f32[384,5]{1,0:T(8,128)}), f32[48,5]{1,0:T(8,128)}) %reduce-scatter.28.cloned.1.call-update) | async-done | bytes 976
  861.8 36.6 %reduce-scatter.26.cloned.1.call-done = f32[48,128]{1,0:T(8,128)} async-done(((f32[384,128]{1,0:T(8,128)}), f32[48,128]{1,0:T(8,128)}) %reduce-scatter.26.cloned.1.call-update) | async-done | bytes 24592 | tf_op jit(solution)/shard_map/reduce_scatter | solution.py:350
  898.4 20.4 %all-reduce.1 = (f32[48,128]{1,0:T(8,128)S(1)}, f32[5,48]{1,0:T(8,128)S(1)}) all-reduce(f32[48,128]{1,0:T(8,128)} %reduce-scatter.26.cloned.1.call-done, f32[5,48]{1,0:T(8,128)S(1)} %copy.181), channel_id=1, replica_groups=mesh['seg'=4,'tm'=8] {'seg'}, use_global_device_ids=true, to_apply=%region_46.47 | all-reduce | flops 6384 | bytes 51072 | tf_op jit(solution)/shard_map/psum | solution.py:353
  920.0 39.9 %all-reduce.5.cloned.1.call-done = (f32[192,384]{1,0:T(8,128)}, f32[48,384]{1,0:T(8,128)}, f32[48,768]{1,0:T(8,128)}, f32[48,384]{1,0:T(8,128)}, f32[48,1536]{1,0:T(8,128)}, /*index=5*/f32[192,384]{1,0:T(8,128)}) async-done(((f32[192,384]{1,0:T(8,128)}, f32[48,384]{1,0:T(8,128)}, f32[48,768]{1,0:T(8,128)}, f32[48,384]{1,0:T(8,128)}, f32[48,1536]{1,0:T(8,128)}, /*index=5*/f32[192,384]{1,0:T(8,128)}), ...) | async-done | bytes 1179664 | tf_op jit(solution)/shard_map/psum | solution.py:353
  974.6 13.5 %psum.87 = f32[]{:T(128)} all-reduce(f32[]{:T(128)S(6)} %add.409), channel_id=1, replica_groups=mesh['seg'=4,'tm'=8] {'tm'}, use_global_device_ids=true, to_apply=%region_56.57 | all-reduce | flops 1 | bytes 8 | tf_op jit(solution)/shard_map/psum | solution.py:360
  (390 shorter events, 157.1 us)
Async XLA Ops:
  7.2 24.5 %copy-start.13 = (bf16[8,128,384]{2,1,0:T(8,128)(2,1)S(1)}, bf16[8,128,384]{2,1,0:T(8,128)(2,1)}, u32[]{:S(2)}) copy-start(bf16[8,128,384]{2,1,0:T(8,128)(2,1)} %param.38) | copy-start | bytes 2359300
  7.2 96.7 %all-gather.6.cloned.1.call-start = ((), (), s32[]{:S(2)}) async-start(), calls=%async_computation.9 | async-start | bytes 1327104 | tf_op jit(solution)/shard_map/all_gather | solution.py:243
  9.0 109.1 %all-gather.8.cloned.1.call-start = ((), (), s32[]{:S(2)}) async-start(), calls=%async_computation.10 | async-start | bytes 14155776 | tf_op jit(solution)/shard_map/all_gather | solution.py:274
  21.7 11.6 %copy-start.86 = (f32[384]{0:T(512)}, f32[384]{0:T(512)S(1)}, u32[]{:S(2)}) copy-start(f32[384]{0:T(512)S(1)} %get-tuple-element.677) | copy-start | bytes 4612
  21.7 90.3 %copy-start.74 = (f32[384]{0:T(512)}, f32[384]{0:T(512)S(1)}, u32[]{:S(2)}) copy-start(f32[384]{0:T(512)S(1)} %get-tuple-element.676) | copy-start | bytes 4612
  21.7 154.7 %copy-start.69 = (f32[384]{0:T(512)}, f32[384]{0:T(512)S(1)}, u32[]{:S(2)}) copy-start(f32[384]{0:T(512)S(1)} %get-tuple-element.678) | copy-start | bytes 4612
  36.0 7.5 copy-start.28
  36.0 8.2 copy-start.96
  36.0 8.3 copy-start.55
  36.0 8.3 copy-start.50
  36.1 8.3 copy-start.48
  36.1 142.4 %all-gather.10.cloned.1.call-start = ((), (), s32[]{:S(2)}) async-start(), calls=%async_computation.11 | async-start | bytes 1327104 | tf_op jit(solution)/shard_map/all_gather | solution.py:247
  36.8 35.6 %copy-start.94 = (s32[8]{0:T(128)S(1)}, s32[8]{0:T(128)}, u32[]{:S(2)}) copy-start(s32[8]{0:T(128)} %param.40) | copy-start | bytes 100
  36.8 160.2 %all-gather.12.cloned.1.call-start = ((), (), s32[]{:S(2)}) async-start(), calls=%async_computation.12 | async-start | bytes 1327104 | tf_op jit(solution)/shard_map/all_gather | solution.py:248
  38.4 45.0 %collective-permute-start.1 = (bf16[8,2,192]{1,2,0:T(8,128)(2,1)}, bf16[8,2,192]{1,2,0:T(8,128)(2,1)}, u32[]{:S(2)}, u32[]{:S(2)}) collective-permute-start(bf16[8,2,192]{1,2,0:T(8,128)(2,1)} %get-tuple-element.779), channel_id=1, source_target_pairs={{1,0},{2,1},{3,2},{4,3},{5,4},{6,5},{7,6},{9,8},{10,9},{11,10},{12... | collective-permute-start | bytes 18440 | tf_op jit(solution)/shard_map/ppermute | solution.py:32
  39.7 43.7 %collective-permute-start = (bf16[8,2,192]{1,2,0:T(8,128)(2,1)S(1)}, bf16[8,2,192]{1,2,0:T(8,128)(2,1)}, u32[]{:S(2)}, u32[]{:S(2)}) collective-permute-start(bf16[8,2,192]{1,2,0:T(8,128)(2,1)S(1)} %get-tuple-element.780), channel_id=1, source_target_pairs={{0,1},{1,2},{2,3},{3,4},{4,5},{5,6},{6,7},{8,9},{9,10},{10,11},{11... | collective-permute-start | bytes 18440 | tf_op jit(solution)/shard_map/ppermute | solution.py:30
  44.2 526.8 %reduce-scatter.16.cloned.1.call-start = ((), (), s32[]{:S(2)}) async-start(), calls=%async_computation.15 | async-start | bytes 28311552 | tf_op jit(solution)/shard_map/reduce_scatter | solution.py:328
  72.5 39.5 %copy-start.36 = (bf16[384,384]{1,0:T(8,128)(2,1)}, bf16[384,384]{1,0:T(8,128)(2,1)S(1)}, u32[]{:S(2)}) copy-start(bf16[384,384]{1,0:T(8,128)(2,1)S(1)} %all_gather.32) | copy-start | bytes 884740
  99.7 2.8 copy-start.20
  178.2 27.1 %copy-start = (f32[1024,384]{0,1:T(8,128)}, f32[1024,384]{0,1:T(8,128)S(1)}, u32[]{:S(2)}) copy-start(f32[1024,384]{0,1:T(8,128)S(1)} %get-tuple-element.766) | copy-start | bytes 4718596
  178.2 90.9 %copy-start.61 = (f32[1024]{0:T(1024)}, f32[1024]{0:T(1024)S(1)}, u32[]{:S(2)}) copy-start(f32[1024]{0:T(1024)S(1)} %broadcast_multiply_fusion) | copy-start | bytes 12292
  178.4 90.7 %copy-start.65 = (f32[1024]{0:T(1024)}, f32[1024]{0:T(1024)S(1)}, u32[]{:S(2)}) copy-start(f32[1024]{0:T(1024)S(1)} %fusion.70) | copy-start | bytes 12292
  250.4 3.6 copy-start.23
  254.1 3.1 copy-start.84
  257.2 9.0 copy-start.1
  257.2 9.0 copy-start.77
  257.2 9.0 copy-start.97
  412.9 195.4 %reduce-scatter.20.cloned.1.call-start = ((), (), s32[]{:S(2)}) async-start(), calls=%async_computation.17 | async-start | bytes 663552 | tf_op jit(solution)/shard_map/reduce_scatter | solution.py:347
  417.0 228.9 %reduce-scatter.14.cloned.1.call-start = ((), (), s32[]{:S(2)}) async-start(), calls=%async_computation.14 | async-start | bytes 663552 | tf_op jit(solution)/shard_map/reduce_scatter | solution.py:345
  419.9 271.7 %reduce-scatter.24.cloned.1.call-start = ((), (), s32[]{:S(2)}) async-start(), calls=%async_computation.19 | async-start | bytes 2654208 | tf_op jit(solution)/shard_map/reduce_scatter | solution.py:349
  425.9 312.0 %reduce-scatter.22.cloned.1.call-start = ((), (), s32[]{:S(2)}) async-start(), calls=%async_computation.18 | async-start | bytes 2654208 | tf_op jit(solution)/shard_map/reduce_scatter | solution.py:348
  433.3 350.3 %reduce-scatter.12.cloned.1.call-start = ((), (), s32[]{:S(2)}) async-start(), calls=%async_computation.13 | async-start | bytes 2654208 | tf_op jit(solution)/shard_map/reduce_scatter | solution.py:344
  435.8 2.6 copy-start.99
  447.5 126.7 %copy-start.14 = (bf16[8,128,384]{2,1,0:T(8,128)(2,1)S(1)}, bf16[8,128,384]{2,1,0:T(8,128)(2,1)}, u32[]{:S(2)}) copy-start(bf16[8,128,384]{2,1,0:T(8,128)(2,1)} %param.38) | copy-start | bytes 2359300
  447.5 126.7 %copy-start.80 = (f32[8,128]{1,0:T(8,128)S(1)}, f32[8,128]{1,0:T(8,128)}, u32[]{:S(2)}) copy-start(f32[8,128]{1,0:T(8,128)} %copy-done.79) | copy-start | bytes 12292
  447.5 126.7 %copy-start.87 = (f32[384]{0:T(512)S(1)}, f32[384]{0:T(512)}, u32[]{:S(2)}) copy-start(f32[384]{0:T(512)} %copy-done.86) | copy-start | bytes 4612
  447.5 126.7 %copy-start.93 = (f32[8,128]{1,0:T(8,128)S(1)}, f32[8,128]{1,0:T(8,128)}, u32[]{:S(2)}) copy-start(f32[8,128]{1,0:T(8,128)} %get-tuple-element.781) | copy-start | bytes 12292
  447.5 376.4 %reduce-scatter.18.cloned.1.call-start = ((), (), s32[]{:S(2)}) async-start(), calls=%async_computation.16 | async-start | bytes 1327104 | tf_op jit(solution)/shard_map/reduce_scatter | solution.py:346
  576.4 284.6 %reduce-scatter.28.cloned.1.call-start = ((), (), s32[]{:S(2)}) async-start(), calls=%async_computation.21 | async-start | bytes 221184
  576.5 3.5 copy-start.11
  576.5 3.5 copy-start.24
  579.9 318.5 %reduce-scatter.26.cloned.1.call-start = ((), (), s32[]{:S(2)}) async-start(), calls=%async_computation.20 | async-start | bytes 221184 | tf_op jit(solution)/shard_map/reduce_scatter | solution.py:350
  581.0 407.8 %copy-start.83 = (f32[5,48]{1,0:T(8,128)S(1)}, f32[5,48]{1,0:T(8,128)}, u32[]{:S(2)}) copy-start(f32[5,48]{1,0:T(8,128)} %param.49) | copy-start | bytes 2884
  581.0 407.8 %copy-start.91 = (f32[5,48]{1,0:T(8,128)S(1)}, f32[5,48]{1,0:T(8,128)}, u32[]{:S(2)}) copy-start(f32[5,48]{1,0:T(8,128)} %param.57) | copy-start | bytes 2884
  581.0 407.8 %copy-start.92 = (f32[5,48]{1,0:T(8,128)S(1)}, f32[5,48]{1,0:T(8,128)}, u32[]{:S(2)}) copy-start(f32[5,48]{1,0:T(8,128)} %param.65) | copy-start | bytes 2884
  581.0 408.5 %copy-start.56 = (f32[48,128]{1,0:T(8,128)S(1)}, f32[48,128]{1,0:T(8,128)}, u32[]{:S(2)}) copy-start(f32[48,128]{1,0:T(8,128)} %param.48) | copy-start | bytes 73732
  581.0 408.5 %copy-start.72 = (f32[48,128]{1,0:T(8,128)S(1)}, f32[48,128]{1,0:T(8,128)}, u32[]{:S(2)}) copy-start(f32[48,128]{1,0:T(8,128)} %param.56) | copy-start | bytes 73732
  581.1 408.4 %copy-start.73 = (f32[48,128]{1,0:T(8,128)S(1)}, f32[48,128]{1,0:T(8,128)}, u32[]{:S(2)}) copy-start(f32[48,128]{1,0:T(8,128)} %param.64) | copy-start | bytes 73732
  581.1 409.1 %copy-start.49 = (f32[48,384]{1,0:T(8,128)S(1)}, f32[48,384]{1,0:T(8,128)}, u32[]{:S(2)}) copy-start(f32[48,384]{1,0:T(8,128)} %param.45) | copy-start | bytes 221188
  581.1 409.1 %copy-start.57 = (f32[48,384]{1,0:T(8,128)S(1)}, f32[48,384]{1,0:T(8,128)}, u32[]{:S(2)}) copy-start(f32[48,384]{1,0:T(8,128)} %param.53) | copy-start | bytes 221188
  581.1 409.1 %copy-start.58 = (f32[48,384]{1,0:T(8,128)S(1)}, f32[48,384]{1,0:T(8,128)}, u32[]{:S(2)}) copy-start(f32[48,384]{1,0:T(8,128)} %param.61) | copy-start | bytes 221188
  581.1 378.7 %all-reduce.5.cloned.1.call-start = ((), (), s32[]{:S(2)}) async-start(), calls=%async_computation.22 | async-start | bytes 2359296 | tf_op jit(solution)/shard_map/psum | solution.py:353
  824.0 167.8 %copy-start.51 = (f32[48,384]{1,0:T(8,128)S(1)}, f32[48,384]{1,0:T(8,128)}, u32[]{:S(2)}) copy-start(f32[48,384]{1,0:T(8,128)} %param.43) | copy-start | bytes 221188
  824.0 167.8 %copy-start.59 = (f32[48,384]{1,0:T(8,128)S(1)}, f32[48,384]{1,0:T(8,128)}, u32[]{:S(2)}) copy-start(f32[48,384]{1,0:T(8,128)} %param.51) | copy-start | bytes 221188
  824.0 167.8 %copy-start.60 = (f32[48,384]{1,0:T(8,128)S(1)}, f32[48,384]{1,0:T(8,128)}, u32[]{:S(2)}) copy-start(f32[48,384]{1,0:T(8,128)} %param.59) | copy-start | bytes 221188
  824.0 168.5 %copy-start.40 = (f32[48,768]{1,0:T(8,128)S(1)}, f32[48,768]{1,0:T(8,128)}, u32[]{:S(2)}) copy-start(f32[48,768]{1,0:T(8,128)} %param.44) | copy-start | bytes 442372
  824.0 168.5 %copy-start.53 = (f32[48,768]{1,0:T(8,128)S(1)}, f32[48,768]{1,0:T(8,128)}, u32[]{:S(2)}) copy-start(f32[48,768]{1,0:T(8,128)} %param.52) | copy-start | bytes 442372
  824.0 168.5 %copy-start.54 = (f32[48,768]{1,0:T(8,128)S(1)}, f32[48,768]{1,0:T(8,128)}, u32[]{:S(2)}) copy-start(f32[48,768]{1,0:T(8,128)} %param.60) | copy-start | bytes 442372
  959.8 31.9 %copy-start.52 = (f32[48,384]{1,0:T(8,128)S(1)}, f32[48,384]{1,0:T(8,128)}, u32[]{:S(2)}) copy-start(f32[48,384]{1,0:T(8,128)} %get-tuple-element.732) | copy-start | bytes 221188
  959.8 32.7 %copy-start.41 = (f32[48,768]{1,0:T(8,128)S(1)}, f32[48,768]{1,0:T(8,128)}, u32[]{:S(2)}) copy-start(f32[48,768]{1,0:T(8,128)} %get-tuple-element.733) | copy-start | bytes 442372
  961.5 31.9 %copy-start.29 = (f32[192,384]{1,0:T(8,128)S(1)}, f32[192,384]{1,0:T(8,128)}, u32[]{:S(2)}) copy-start(f32[192,384]{1,0:T(8,128)} %param.47) | copy-start | bytes 884740
  961.5 31.9 %copy-start.35 = (f32[192,384]{1,0:T(8,128)S(1)}, f32[192,384]{1,0:T(8,128)}, u32[]{:S(2)}) copy-start(f32[192,384]{1,0:T(8,128)} %get-tuple-element.736) | copy-start | bytes 884740
  961.5 31.9 %copy-start.42 = (f32[192,384]{1,0:T(8,128)S(1)}, f32[192,384]{1,0:T(8,128)}, u32[]{:S(2)}) copy-start(f32[192,384]{1,0:T(8,128)} %param.55) | copy-start | bytes 884740
  961.5 31.9 %copy-start.43 = (f32[192,384]{1,0:T(8,128)S(1)}, f32[192,384]{1,0:T(8,128)}, u32[]{:S(2)}) copy-start(f32[192,384]{1,0:T(8,128)} %param.63) | copy-start | bytes 884740
  (52 other events, 91.3 us)
Sparse Core Ops, SparseCore 0:
  10.5 26.7 all-gather.5
  39.2 78.8 all-gather.7
  120.5 24.0 all-gather.9
  146.9 24.0 all-gather.11
  413.1 157.8 reduce-scatter.15
  573.9 34.3 reduce-scatter.19
  611.4 34.3 reduce-scatter.13
  649.2 42.4 reduce-scatter.23
  695.4 42.4 reduce-scatter.21
  741.1 42.4 reduce-scatter.11
  787.2 36.7 reduce-scatter.17
  827.4 33.4 reduce-scatter.27
  864.8 33.5 reduce-scatter.25
  901.1 58.6 all-reduce.4
where the time goes:
time: 1010 us; the launch traced here: 1000 us
  waiting for transfers between devices  484 us (48%)
  matrix products  152 us (15%)
  local copies, waits for them, and re-layouts  142 us (14%)
  blocking collectives  131 us (13%)
  other arithmetic  65.4 us (6%)
  between operations  23 us (2%)
    reduce_scatter x1, waiting for transfers between devices, on_device(): lax.psum_scatter(keyval_grad_all, 'tm', scatter_dimension=1, tiled=True)  123 us
    dynamic_update_slice x8, local copies, waits for them, and re-layouts, grad_step(): lax.dynamic_update_slice_in_dim(keyval_grad, joined, position * block_siz...  50.2 us
    reduce_scatter x1, waiting for transfers between devices, on_device(): lax.psum_scatter(grad_up, 'tm', scatter_dimension=0, tiled=True)  46.2 us
    reduce_scatter x1, waiting for transfers between devices, on_device(): lax.psum_scatter(grad_down, 'tm', scatter_dimension=0, tiled=True)  45.8 us
    reduce_scatter x1, waiting for transfers between devices, on_device(): lax.psum_scatter(grad_conv, 'tm', scatter_dimension=0, tiled=True)  45.7 us
    reduce_scatter x1, waiting for transfers between devices, on_device(): lax.psum_scatter(grad_keyval, 'tm', scatter_dimension=0, tiled=True)  40.4 us
    psum x1, waiting for transfers between devices, on_device(): lax.psum((shards[0], shards[1], shards[2], shards[3], shards[4], shards[5...  39.9 us
    psum x1, blocking collectives, on_device(): loss_sum, sample_count = lax.psum((loss_part, count_part), ('seg', 'tm'))  39.5 us
  transfers between devices with their start and end apart: 16, of which 11 were waited for; matrix products, arithmetic and copies ran while one was open for 15% of the time, Pallas kernels for 0%

commit v1 on v0

v1 whole, which is shorter than its diff:
```python
import functools
import jax
import jax.numpy as jnp
from jax import lax
from jax.experimental import pallas as pl
from jax.experimental.pallas import tpu as pltpu
from jax.sharding import PartitionSpec as P

H = 8
STEMS = 4
SUB = 16
STEP = 10
LANES = 128

clip_limit = 0.001
beta_first = 0.9
beta_second = 0.999
learn_rate = 0.03
fast_rate = 0.5
weight_decay = 0.05
adam_epsilon = 1e-08
norm_epsilon = 1e-05

bfloat = jnp.bfloat16
float32 = jnp.float32
VMEM_LIMIT = 60 * 1024 * 1024


def mm(left, right):
    return lax.dot_general(left, right, (((1,), (0,)), ((), ())), preferred_element_type=float32)


def nt(left, right):
    return lax.dot_general(left, right, (((1,), (1,)), ((), ())), preferred_element_type=float32)


def tn(left, right):
    return lax.dot_general(left, right, (((0,), (0,)), ((), ())), preferred_element_type=float32)


def iota(shape, dim):
    return lax.broadcasted_iota(jnp.int32, shape, dim)


def norm_parts(values):
    centred = values - jnp.mean(values, -1, keepdims=True)
    scale = lax.rsqrt(jnp.mean(centred * centred, -1, keepdims=True) + norm_epsilon)
    return centred * scale, scale


def norm_back(unit, scale, gain, upstream):
    inner = upstream * gain
    value_grad = scale * (
        inner
        - jnp.mean(inner, -1, keepdims=True)
        - unit * jnp.mean(inner * unit, -1, keepdims=True)
    )
    return value_grad, jnp.sum(upstream * unit, 0, keepdims=True)


def gelu_both(values):
    upper = 0.5 * (1.0 + lax.erf(values * 0.7071067811865476))
    density = jnp.exp(-0.5 * values * values) * 0.3989422804014327
    return values * upper, upper + values * density


def spread_matrix(width, head_size):
    shape = (width, width // head_size * LANES)
    lane = iota(shape, 1)
    inside = lane % LANES
    source = (lane // LANES) * head_size + inside
    hit = jnp.logical_and(iota(shape, 0) == source, inside < head_size)
    return jnp.where(hit, 1.0, 0.0).astype(bfloat)


def with_column(block, column, head_size):
    lane = iota(block.shape, 1)
    high = column.astype(bfloat).astype(float32)
    rest = column - high
    middle = rest.astype(bfloat).astype(float32)
    low = rest - middle
    pieces = jnp.where(lane == head_size, high, jnp.where(lane == head_size + 1, middle, low))
    spare = jnp.logical_and(lane >= head_size, lane < head_size + 3)
    return jnp.where(spare, pieces, block.astype(float32)).astype(bfloat)


class Sizes:
    def __init__(self, n, feats, spectral, target, conv_weight, up_weight):
        self.n = n
        self.segments = feats.shape[0]
        self.parts = n // self.segments
        self.tokens_dev = spectral.shape[1]
        self.D = spectral.shape[2]
        self.taps = conv_weight.shape[0] * n
        self.frame = self.taps // 2
        self.F = up_weight.shape[1]
        self.out = target.shape[2]
        self.tokens = self.segments * self.tokens_dev
        self.keys = self.tokens * self.parts
        self.hd = self.D // H
        self.wide = H * LANES
        self.w = self.D // n
        self.cw = self.taps // n
        self.uw = self.w * (self.F // self.D)
        self.fw = self.F // n
        self.hw = self.w * self.out // self.D
        self.direct = self.parts == 1 and self.w % 16 == 0 and self.hw % 16 == 0 and self.hw > 0
        self.first_rows = self.cw + 3 * self.w + 16
        self.second_rows = self.w + self.uw + self.fw + self.hw
        self.block = 256
        self.query_block = 256 if self.keys <= 1024 else 128


def pack_weights(z, tm_place, conv, query, keyval, out, up, down, head, gains):
    D, w = z.D, z.w

    def kernel(place_ref, conv_r, query_r, keyval_r, out_r, up_r, down_r, head_r, gains_r, o_ref):
        row = 0

        def put(value):
            nonlocal row
            o_ref[row : row + value.shape[0], :] = value.astype(bfloat)
            row += value.shape[0]

        put(conv_r[...])
        put(query_r[...])
        put(keyval_r[:, :D])
        put(keyval_r[:, D:])
        start = place_ref[0] * w
        shift = jnp.where(iota((w, D), 1) == iota((w, D), 0) + start, 1.0, 0.0).astype(bfloat)
        placed = mm(gains_r[...].astype(bfloat), shift)
        put(jnp.concatenate([placed, jnp.zeros((16 - placed.shape[0], D), float32)], 0))
        put(out_r[...])
        for c in range(z.F // D):
            put(up_r[:, c * D : (c + 1) * D])
        put(down_r[...])
        rows = z.hw
        put(jnp.concatenate([head_r[g * rows : (g + 1) * rows, :] for g in range(D // z.out)], 1))

    vmem = pl.BlockSpec(memory_space=pltpu.VMEM)
    return pl.pallas_call(
        kernel,
        out_shape=jax.ShapeDtypeStruct((z.first_rows + z.second_rows, D), bfloat),
        in_specs=[pl.BlockSpec(memory_space=pltpu.SMEM)] + [vmem] * 8,
        out_specs=vmem,
        name="pack_weights",
    )(tm_place, conv, query, keyval, out, up, down, head, gains)


def pack_tokens(z, feats, spectral, target):
    channels = feats.shape[2]
    rows = z.tokens_dev
    width = z.frame + z.D + z.out

    def kernel(f_ref, s_ref, t_ref, o_ref, scratch):
        frames = f_ref[0].astype(float32)
        pieces = []
        for c in range(0, channels, LANES):
            scratch[c // LANES, :, : min(LANES, channels - c)] = frames[:, c : c + LANES]
        for j in range(4):
            for c in range(0, channels, LANES):
                piece = scratch[c // LANES, pl.ds(j, rows, stride=4), :]
                pieces.append(piece[:, : min(LANES, channels - c)])
        o_ref[0, :, : z.frame] = jnp.concatenate(pieces, 1).astype(bfloat)
        o_ref[0, :, z.frame : z.frame + z.D] = s_ref[0]
        o_ref[0, :, z.frame + z.D :] = t_ref[0]

    return pl.pallas_call(
        kernel,
        grid=(z.segments,),
        out_shape=jax.ShapeDtypeStruct((z.segments, rows, width), bfloat),
        in_specs=[
            pl.BlockSpec((1, 4 * rows, channels), lambda i: (i, 0, 0)),
            pl.BlockSpec((1, rows, z.D), lambda i: (i, 0, 0)),
            pl.BlockSpec((1, rows, z.out), lambda i: (i, 0, 0)),
        ],
        out_specs=pl.BlockSpec((1, rows, width), lambda i: (i, 0, 0)),
        scratch_shapes=[pltpu.VMEM((pl.cdiv(channels, LANES), 4 * rows, LANES), float32)],
        name="pack_tokens",
    )(feats, spectral, target)


def front(z, moved, spectral_all, halo, weights):
    D, T, K, W, B = z.D, z.tokens, z.keys, z.wide, z.block
    frame, taps, hd = z.frame, z.taps, z.hd
    half = frame // 2
    QB = z.query_block

    def kernel(*refs):
        refs = list(refs)
        x_ref, sp_ref = refs[:2]
        refs = refs[2:]
        if z.parts > 1:
            before_ref, after_ref = refs[:2]
            refs = refs[2:]
        if z.direct:
            blob_ref = refs[0]
            refs = refs[1:]
        else:
            wc, wq, wkv, gains_ref = refs[:4]
            refs = refs[4:]
        (stream_o, slope_o, normed_o, sn_o, q_o, k_o, v_o, att_o) = refs[:8]
        refs = refs[8:]
        conv_s, wq_s, wk_s, wv_s = refs[:4]
        refs = refs[4:]
        if z.direct:
            blob_s, wc, wqkv, sem = refs
            copy = pltpu.make_async_copy(blob_ref.at[:, 0 : z.first_rows], blob_s, sem)
            copy.start()
            copy.wait()
            w, cw = z.w, z.cw
            total = jnp.zeros((16, D), float32)
            for j in range(z.n):
                wc[j * cw : (j + 1) * cw, :] = blob_s[j, 0:cw, :]
                for c in range(3):
                    first = cw + c * w
                    wqkv[j * w : (j + 1) * w, c * D : (c + 1) * D] = blob_s[j, first : first + w, :]
                total = total + blob_s[j, cw + 3 * w : cw + 3 * w + 16, :].astype(float32)
            gain_query, gain_keys = total[0:1, :], total[1:2, :]
            parts_w = [wqkv[:, c * D : (c + 1) * D] for c in range(3)]
        else:
            gain_query, gain_keys = gains_ref[0:1, :], gains_ref[1:2, :]
            parts_w = [wq[...], wkv[:, :D], wkv[:, D:]]
        spread = spread_matrix(D, hd)
        for target_s, part in zip((wq_s, wk_s, wv_s), parts_w):
            target_s[...] = mm(part, spread).astype(bfloat)

        conv_s[...] = mm(x_ref[...], wc[half : half + frame, :])
        row = iota((T, D), 0)
        older = pltpu.roll(mm(x_ref[:, half:], wc[:half, :]), 1, 0)
        first_row, last_row = 0.0, 0.0
        if z.parts > 1:
            first_row = mm(before_ref[...], wc[:half, :])[0:1, :]
            last_row = mm(after_ref[...], wc[half + frame :, :])[0:1, :]
        conv_s[...] += jnp.where(row == 0, first_row, older)
        newer = pltpu.roll(mm(x_ref[:, :half], wc[half + frame :, :]), T - 1, 0)
        conv_s[...] += jnp.where(row == T - 1, last_row, newer)

        def token_block(i, carry):
            rows = pl.ds(pl.multiple_of(i * B, B), B)
            stream, slope = gelu_both(conv_s[rows, :])
            stream_o[rows, :] = stream
            slope_o[rows, :] = slope
            unit, _ = norm_parts(stream)
            normed = (unit * gain_query).astype(bfloat)
            normed_o[rows, :] = normed
            q_o[rows, :] = mm(normed, wq_s[...]).astype(bfloat)
            return carry

        lax.fori_loop(0, T // B, token_block, 0)

        def key_block(i, carry):
            rows = pl.ds(pl.multiple_of(i * B, B), B)
            unit, _ = norm_parts(sp_ref[rows, :].astype(float32))
            normed = (unit * gain_keys).astype(bfloat)
            sn_o[rows, :] = normed
            inside = iota((B, W), 1) % LANES
            spare = jnp.logical_and(inside >= hd, inside < hd + 3)
            k_o[rows, :] = jnp.where(spare, -1.0, mm(normed, wk_s[...])).astype(bfloat)
            v_o[rows, :] = jnp.where(spare, -1.0, mm(normed, wv_s[...])).astype(bfloat)
            return carry

        lax.fori_loop(0, K // B, key_block, 0)

        def head(h, carry):
            lanes = pl.ds(pl.multiple_of(h * LANES, LANES), LANES)
            for b in range(T // QB):
                rows = slice(b * QB, (b + 1) * QB)
                q = q_o[rows, lanes]
                scores = nt(q, k_o[:, lanes])
                top = jnp.max(scores, -1, keepdims=True)
                grown = jnp.exp(scores - top)
                mass = jnp.sum(grown, -1, keepdims=True)
                probs = (grown * (1.0 / mass)).astype(bfloat)
                att_o[rows, lanes] = mm(probs, v_o[:, lanes]).astype(bfloat)
                q_o[rows, lanes] = with_column(q, top + jnp.log(mass), hd)
            return carry

        lax.fori_loop(0, H, head, 0)

    vmem = pl.BlockSpec(memory_space=pltpu.VMEM)
    in_specs = [pl.BlockSpec((T, frame), lambda i: (0, 0))]
    args = [moved]
    if z.parts > 1:
        args += [spectral_all, halo[0], halo[1]]
        in_specs += [pl.BlockSpec((K, D), lambda i: (0, 0))] + [pl.BlockSpec((16, D), lambda i: (0, 0))] * 2
    else:
        args.append(moved)
        in_specs.append(pl.BlockSpec((T, D), lambda i: (0, frame // D)))
    scratch = [
        pltpu.VMEM((T, D), float32),
        pltpu.VMEM((D, W), bfloat),
        pltpu.VMEM((D, W), bfloat),
        pltpu.VMEM((D, W), bfloat),
    ]
    if z.direct:
        args.append(weights[0])
        in_specs.append(pl.BlockSpec(memory_space=pl.ANY))
        scratch += [
            pltpu.VMEM((z.n, z.first_rows, D), bfloat),
            pltpu.VMEM((taps, D), bfloat),
            pltpu.VMEM((D, 3 * D), bfloat),
            pltpu.SemaphoreType.DMA,
        ]
    else:
        for array in (weights[0], weights[1], weights[2], weights[7]):
            args.append(array)
            in_specs.append(pl.BlockSpec(array.shape, lambda i: (0, 0)))
    shapes = [
        ((T, D), float32),
        ((T, D), float32),
        ((T, D), bfloat),
        ((K, D), bfloat),
        ((T, W), bfloat),
        ((K, W), bfloat),
        ((K, W), bfloat),
        ((T, W), bfloat),
    ]
    return pl.pallas_call(
        kernel,
        grid=(1,),
        out_shape=[jax.ShapeDtypeStruct(s, d) for s, d in shapes],
        in_specs=in_specs,
        out_specs=[pl.BlockSpec(s, lambda i: (0, 0)) for s, d in shapes],
        scratch_shapes=scratch,
        compiler_params=pltpu.CompilerParams(vmem_limit_bytes=VMEM_LIMIT),
        cost_estimate=pl.CostEstimate(flops=30_000_000_000, bytes_accessed=20_000_000, transcendentals=10_000_000),
        name="front",
    )(*args)


def emit_blocks(z, meta_ref, keep_o, send_o, sources):
    chip, core = meta_ref[6], meta_ref[7]
    for m in range(z.n // 2):
        owner = (chip ^ m) * 2
        for out, place in ((keep_o, owner + core), (send_o, owner + 1 - core)):
            row = 0
            for ref, rows, pieces in sources:
                for lane in range(0, ref.shape[-1], z.D):
                    if ref.shape[-1] >= z.D:
                        here = ref[pl.ds(pl.multiple_of(place * rows, 16), rows), lane : lane + z.D]
                        out[m, row : row + rows, :] = here.astype(out.dtype)
                        row += rows
                    else:
                        size = rows // pieces
                        for g in range(pieces):
                            start = pl.multiple_of(place * rows + g * size, 16)
                            here = ref[pl.ds(start, size), :]
                            lanes = slice(g * ref.shape[-1], (g + 1) * ref.shape[-1])
                            out[m, row : row + size, lanes] = here.astype(out.dtype)
                        row += size


def middle(z, meta, count, stream, att, moved, target, weights):
    D, T, W, B, F, O = z.D, z.tokens, z.wide, z.block, z.F, z.out
    hd = z.hd

    def kernel(meta_ref, count_ref, stream_ref, att_ref, target_ref, *refs):
        refs = list(refs)
        if z.direct:
            blob_ref = refs[0]
            refs = refs[1:]
        else:
            wo, wu, wd, wh, gains_ref = refs[:5]
            refs = refs[5:]
        if z.direct:
            do_o, mid_o, misc_o, keep_o, send_o = refs[:5]
            refs = refs[5:]
        else:
            do_o, mid_o, misc_o, go_o, gu_o, gd_o, gh_o = refs[:7]
            refs = refs[7:]
        wop, act_s, hg_s, fin_s, fg_s, low_s, pg_s, bg_s, go_s, gu_s, gd_s, gh_s = refs[:12]
        refs = refs[12:]
        if z.direct:
            blob_s, gain_s, wo, wu, wd, wh, sem, sem2 = refs
            w, uw, fw, hw = z.w, z.uw, z.fw, z.hw
            copy = pltpu.make_async_copy(blob_ref.at[:, z.first_rows :], blob_s, sem)
            copy.start()
            copy2 = pltpu.make_async_copy(blob_ref.at[:, z.first_rows - 16 : z.first_rows], gain_s, sem2)
            copy2.start()
            copy.wait()
            copy2.wait()
            total = jnp.zeros((16, D), float32)
            for j in range(z.n):
                wo[j * w : (j + 1) * w, :] = blob_s[j, 0:w, :]
                for c in range(F // D):
                    first = w + c * w
                    wu[j * w : (j + 1) * w, c * D : (c + 1) * D] = blob_s[j, first : first + w, :]
                wd[j * fw : (j + 1) * fw, :] = blob_s[j, w + uw : w + uw + fw, :]
                for g in range(D // O):
                    start = j * w + g * hw
                    wh[start : start + hw, :] = blob_s[j, w + uw + fw :, g * O : (g + 1) * O]
                total = total + gain_s[j].astype(float32)
        else:
            total = gains_ref[...]
        gain_ffn, scale_attn, scale_ffn = total[2:3, :], total[3:4, :], total[4:5, :]
        spread = spread_matrix(D, hd)
        wop[...] = tn(spread, wo[...]).astype(bfloat)
        misc_o[...] = jnp.zeros_like(misc_o)
        base, valid = meta_ref[0], meta_ref[1]
        samples = count_ref[0]

        def block(i, carry):
            rows = pl.ds(pl.multiple_of(i * B, B), B)
            att = att_ref[rows, :]
            branch = mm(att, wop[...])
            stream_mid = stream_ref[rows, :] + scale_attn * branch
            unit, scale = norm_parts(stream_mid)
            ffn_in = (unit * gain_ffn).astype(bfloat)
            fin_s[rows, :] = ffn_in
            hidden = mm(ffn_in, wu[...])
            active, slope = gelu_both(hidden)
            active = active.astype(bfloat)
            act_s[rows, :] = active
            ffn_out = mm(active, wd[...])
            stream_low = (stream_mid + scale_ffn * ffn_out).astype(bfloat)
            low_s[rows, :] = stream_low
            predicted = mm(stream_low, wh[...])
            column = iota((B, O), 1)
            position = (base + i * B + iota((B, O), 0)) * SUB + column % SUB
            stem = column // (2 * SUB)
            weight = jnp.zeros((B, O), float32)
            for k in range(STEMS):
                weight = jnp.where(stem == k, meta_ref[2 + k].astype(float32), weight)
            weight = jnp.where(position < valid, weight, 0.0)
            error = predicted - target_ref[rows, :].astype(float32)
            root = jnp.sqrt(error * error + 1.0)
            misc_o[5:6, :O] += jnp.sum(weight * (root - 1.0), 0, keepdims=True)
            predicted_grad = (weight * error / root / samples).astype(bfloat)
            pg_s[rows, :] = predicted_grad
            end_grad = nt(predicted_grad, wh[...])
            misc_o[4:5, :] += jnp.sum(end_grad * ffn_out, 0, keepdims=True)
            ffn_grad = (scale_ffn * end_grad).astype(bfloat)
            fg_s[rows, :] = ffn_grad
            hidden_grad = (nt(ffn_grad, wd[...]) * slope).astype(bfloat)
            hg_s[rows, :] = hidden_grad
            mid_part, gain_grad = norm_back(unit, scale, gain_ffn, nt(hidden_grad, wu[...]))
            misc_o[2:3, :] += gain_grad
            mid_grad = end_grad + mid_part
            mid_o[rows, :] = mid_grad
            misc_o[3:4, :] += jnp.sum(mid_grad * branch, 0, keepdims=True)
            branch_grad = (scale_attn * mid_grad).astype(bfloat)
            bg_s[rows, :] = branch_grad
            att_grad = nt(branch_grad, wop[...]).astype(bfloat)
            for h in range(H):
                lanes = slice(h * LANES, (h + 1) * LANES)
                one = att_grad[:, lanes].astype(float32)
                delta = jnp.sum(one * att[:, lanes].astype(float32), -1, keepdims=True)
                do_o[rows, lanes] = with_column(one, delta, hd)
            return carry

        lax.fori_loop(0, T // B, block, 0)
        spare_grad = tn(att_ref[...], bg_s[...])
        for h in range(H):
            go_s[h * hd : (h + 1) * hd, :] = spare_grad[h * LANES : h * LANES + hd, :]
        gu_s[...] = tn(fin_s[...], hg_s[...])
        gd_s[...] = tn(act_s[...], fg_s[...])
        gh_s[...] = tn(low_s[...], pg_s[...])
        if z.direct:
            emit_blocks(
                z,
                meta_ref,
                keep_o,
                send_o,
                ((go_s, z.w, 1), (gu_s, z.w, 1), (gd_s, z.fw, 1), (gh_s, z.w, D // O)),
            )
        else:
            go_o[...] = go_s[...]
            gu_o[...] = gu_s[...]
            gd_o[...] = gd_s[...]
            gh_o[...] = gh_s[...]

    def whole(shape):
        return pl.BlockSpec(shape, lambda i: (0,) * len(shape))

    smem = pl.BlockSpec(memory_space=pltpu.SMEM)
    in_specs = [smem, smem, whole((T, D)), whole((T, W))]
    args = [meta, count, stream, att, target]
    in_specs.append(pl.BlockSpec((T, O), lambda i: (0, (z.frame + D) // O)))
    scratch = [
        pltpu.VMEM((W, D), bfloat),
        pltpu.VMEM((T, F), bfloat),
        pltpu.VMEM((T, F), bfloat),
        pltpu.VMEM((T, D), bfloat),
        pltpu.VMEM((T, D), bfloat),
        pltpu.VMEM((T, D), bfloat),
        pltpu.VMEM((T, O), bfloat),
        pltpu.VMEM((T, D), bfloat),
        pltpu.VMEM((D, D), float32),
        pltpu.VMEM((D, F), float32),
        pltpu.VMEM((F, D), float32),
        pltpu.VMEM((D, O), float32),
    ]
    shapes = [((T, W), bfloat), ((T, D), float32), ((8, D), float32)]
    if z.direct:
        args.append(weights[0])
        in_specs.append(pl.BlockSpec(memory_space=pl.ANY))
        scratch += [
            pltpu.VMEM((z.n, z.second_rows, D), bfloat),
            pltpu.VMEM((z.n, 16, D), bfloat),
            pltpu.VMEM((D, D), bfloat),
            pltpu.VMEM((D, F), bfloat),
            pltpu.VMEM((F, D), bfloat),
            pltpu.VMEM((D, O), bfloat),
            pltpu.SemaphoreType.DMA,
            pltpu.SemaphoreType.DMA,
        ]
        shapes += [
            ((z.n // 2, z.second_rows, D), float32),
            ((z.n // 2, z.second_rows, D), bfloat),
        ]
    else:
        for array in (weights[3], weights[4], weights[5], weights[6], weights[7]):
            args.append(array)
            in_specs.append(whole(array.shape))
        shapes += [((D, D), float32), ((D, F), float32), ((F, D), float32), ((D, O), float32)]
    return pl.pallas_call(
        kernel,
        grid=(1,),
        out_shape=[jax.ShapeDtypeStruct(s, d) for s, d in shapes],
        in_specs=in_specs,
        out_specs=[whole(s) for s, d in shapes],
        scratch_shapes=scratch,
        compiler_params=pltpu.CompilerParams(vmem_limit_bytes=VMEM_LIMIT),
        cost_estimate=pl.CostEstimate(flops=15_000_000_000, bytes_accessed=20_000_000, transcendentals=4_000_000),
        name="middle",
    )(*args)


def attend_back(z, q, k, v, do):
    T, K, W, D = z.tokens, z.keys, z.wide, z.D
    hd, QB = z.hd, z.query_block

    def kernel(q_ref, k_ref, v_ref, do_ref, dq_o, dkv_o):
        for b in range(T // QB):
            rows = slice(b * QB, (b + 1) * QB)
            q, do = q_ref[rows, :], do_ref[rows, :]
            probs = jnp.exp(nt(q, k_ref[...]))
            score_grad = (probs * nt(do, v_ref[...])).astype(bfloat)
            low = probs.astype(bfloat)
            dq_o[rows, :] = mm(score_grad, k_ref[...]).astype(bfloat)
            dk = tn(q, score_grad)
            dv = tn(do, low)
            if b == 0:
                dk_sum, dv_sum = dk, dv
            else:
                dk_sum, dv_sum = dk_sum + dk, dv_sum + dv
        dkv_o[0] = dk_sum[:hd, :].astype(bfloat)
        dkv_o[1] = dv_sum[:hd, :].astype(bfloat)

    def lanes(rows):
        return pl.BlockSpec((rows, LANES), lambda h: (0, h))

    return pl.pallas_call(
        kernel,
        grid=(H,),
        out_shape=[
            jax.ShapeDtypeStruct((T, W), bfloat),
            jax.ShapeDtypeStruct((2, D, K), bfloat),
        ],
        in_specs=[lanes(T), lanes(K), lanes(K), lanes(T)],
        out_specs=[lanes(T), pl.BlockSpec((2, hd, K), lambda h: (0, h, 0))],
        compiler_params=pltpu.CompilerParams(vmem_limit_bytes=VMEM_LIMIT),
        cost_estimate=pl.CostEstimate(flops=40_000_000_000, bytes_accessed=12_000_000, transcendentals=10_000_000),
        name="attend_back",
    )(q, k, v, do)


def back(z, meta, moved, spectral_all, halo, stream, slope, normed, sn, mid, dq, dkv, misc, weights):
    D, T, K, W, B, O = z.D, z.tokens, z.keys, z.wide, z.block, z.out
    frame, taps, hd = z.frame, z.taps, z.hd
    half = frame // 2

    def kernel(meta_ref, x_ref, sp_ref, stream_ref, slope_ref, normed_ref, sn_ref, mid_ref, dq_ref, dkv_ref, misc_ref, *refs):
        refs = list(refs)
        if z.parts > 1:
            before_ref, after_ref = refs[:2]
            refs = refs[2:]
        if z.direct:
            blob_ref = refs[0]
            keep_o, send_o = refs[1:3]
            refs = refs[3:]
        else:
            wq, wkv, gains_ref = refs[:3]
            gc_o, gq_o, gkv_o, misc_o = refs[3:7]
            refs = refs[7:]
        gc_s, gq_s, gkv_s, misc_s, cg_s, dqc_s, dkvt_s = refs[:7]
        refs = refs[7:]
        if z.direct:
            blob_s, wq, wkv, place_s, sem = refs
            w, cw = z.w, z.cw
            copy = pltpu.make_async_copy(blob_ref.at[:, cw : z.first_rows], blob_s, sem)
            copy.start()
            copy.wait()
            total = jnp.zeros((16, D), float32)
            for j in range(z.n):
                here = slice(j * w, (j + 1) * w)
                wq[here, :] = blob_s[j, 0:w, :]
                wkv[here, :D] = blob_s[j, w : 2 * w, :]
                wkv[here, D:] = blob_s[j, 2 * w : 3 * w, :]
                total = total + blob_s[j, 3 * w :, :].astype(float32)
        else:
            total = gains_ref[...]
        gain_query = total[0:1, :]
        misc_s[...] = misc_ref[...]
        spread = spread_matrix(D, hd)
        dqc_s[...] = nt(dq_ref[...], spread).astype(bfloat)
        dkvt_s[:, :D] = dkv_ref[0].T
        dkvt_s[:, D:] = dkv_ref[1].T
        gkv_s[...] = tn(sn_ref[...], dkvt_s[...])
        gq_s[...] = tn(normed_ref[...], dqc_s[...])

        def key_block(i, carry):
            rows = pl.ds(pl.multiple_of(i * B, B), B)
            unit, _ = norm_parts(sp_ref[rows, :].astype(float32))
            misc_s[1:2, :] += jnp.sum(nt(dkvt_s[rows, :], wkv[...]) * unit, 0, keepdims=True)
            return carry

        lax.fori_loop(0, K // B, key_block, 0)

        def token_block(i, carry):
            rows = pl.ds(pl.multiple_of(i * B, B), B)
            unit, scale = norm_parts(stream_ref[rows, :])
            part, gain_grad = norm_back(unit, scale, gain_query, nt(dqc_s[rows, :], wq[...]))
            misc_s[0:1, :] += gain_grad
            conv_grad = (mid_ref[rows, :] + part) * slope_ref[rows, :]
            cg_s[rows, :] = conv_grad.astype(bfloat).astype(float32)
            return carry

        lax.fori_loop(0, T // B, token_block, 0)
        conv_grad = cg_s[...]
        gc_s[half : half + frame, :] = tn(x_ref[...], conv_grad.astype(bfloat))
        row = iota((T, D), 0)
        later = jnp.where(row == T - 1, 0.0, pltpu.roll(conv_grad, T - 1, 0)).astype(bfloat)
        gc_s[:half, :] = tn(x_ref[:, half:], later)
        sooner = jnp.where(row == 0, 0.0, pltpu.roll(conv_grad, 1, 0)).astype(bfloat)
        gc_s[half + frame :, :] = tn(x_ref[:, :half], sooner)
        if z.parts > 1:
            top = jnp.where(iota((16, D), 0) == 0, conv_grad[0:16, :], 0.0).astype(bfloat)
            gc_s[:half, :] += tn(before_ref[...], top)
            tail = jnp.where(iota((16, D), 0) == 0, pltpu.roll(conv_grad[T - 16 :, :], 1, 0), 0.0)
            gc_s[half + frame :, :] += tn(after_ref[...], tail.astype(bfloat))
        if z.direct:
            for j in range(z.n):
                pick = jnp.where(iota((D, LANES), 0) == iota((D, LANES), 1) + j * z.w, 1.0, 0.0)
                pick = jnp.where(iota((D, LANES), 1) < z.w, pick, 0.0)
                chosen = lax.dot_general(
                    misc_s[...], pick, (((1,), (0,)), ((), ())),
                    precision=lax.Precision.HIGHEST, preferred_element_type=float32,
                )
                low_rows = jnp.where(iota((8, LANES), 0) == 5, misc_s[:, :LANES], chosen)
                place_s[j * 16 : (j + 1) * 16, :] = jnp.zeros((16, D), float32)
                place_s[j * 16 : j * 16 + 8, :LANES] = low_rows
            emit_blocks(
                z, meta_ref, keep_o, send_o,
                ((gc_s, z.cw, 1), (gq_s, z.w, 1), (gkv_s, z.w, 1), (place_s, 16, 1)),
            )
        else:
            gc_o[...] = gc_s[...]
            gq_o[...] = gq_s[...]
            gkv_o[...] = gkv_s[...]
            misc_o[...] = misc_s[...]

    def whole(shape):
        return pl.BlockSpec(shape, lambda i: (0,) * len(shape))

    args = [meta, moved, moved if z.parts == 1 else spectral_all]
    in_specs = [
        pl.BlockSpec(memory_space=pltpu.SMEM),
        whole((T, frame)),
        pl.BlockSpec((T, D), lambda i: (0, frame // D)) if z.parts == 1 else whole((K, D)),
    ]
    for array in (stream, slope, normed, sn, mid, dq, dkv, misc):
        args.append(array)
        in_specs.append(whole(array.shape))
    if z.parts > 1:
        args += list(halo)
        in_specs += [whole((16, D))] * 2
    scratch = [
        pltpu.VMEM((taps, D), float32),
        pltpu.VMEM((D, D), float32),
        pltpu.VMEM((D, 2 * D), float32),
        pltpu.VMEM((8, D), float32),
        pltpu.VMEM((T, D), float32),
        pltpu.VMEM((T, D), bfloat),
        pltpu.VMEM((K, 2 * D), bfloat),
    ]
    if z.direct:
        args.append(weights[0])
        in_specs.append(pl.BlockSpec(memory_space=pl.ANY))
        scratch += [
            pltpu.VMEM((z.n, z.first_rows - z.cw, D), bfloat),
            pltpu.VMEM((D, D), bfloat),
            pltpu.VMEM((D, 2 * D), bfloat),
            pltpu.VMEM((z.n * 16, D), float32),
            pltpu.SemaphoreType.DMA,
        ]
        shapes = [
            ((z.n // 2, z.first_rows, D), float32),
            ((z.n // 2, z.first_rows, D), bfloat),
        ]
    else:
        for array in (weights[1], weights[2], weights[7]):
            args.append(array)
            in_specs.append(whole(array.shape))
        shapes = [((taps, D), float32), ((D, D), float32), ((D, 2 * D), float32), ((8, D), float32)]
    return pl.pallas_call(
        kernel,
        grid=(1,),
        out_shape=[jax.ShapeDtypeStruct(s, d) for s, d in shapes],
        in_specs=in_specs,
        out_specs=[whole(s) for s, d in shapes],
        scratch_shapes=scratch,
        compiler_params=pltpu.CompilerParams(vmem_limit_bytes=VMEM_LIMIT),
        cost_estimate=pl.CostEstimate(flops=12_000_000_000, bytes_accessed=20_000_000, transcendentals=10_000),
        name="back",
    )(*args)


def pairs(count, mask):
    return [(i, i ^ mask) for i in range(count)]


def tree_sum(values):
    while len(values) > 1:
        values = [values[i] + values[i + 1] for i in range(0, len(values), 2)]
    return values[0]


def reduce_blocks(z, keep, send, planes):
    blocks = keep + lax.ppermute(send, "tm", pairs(z.n, 1)).astype(float32)
    mine = [blocks[0]]
    for m in range(1, z.n // 2):
        there = lax.ppermute(blocks[m].astype(bfloat), "tm", pairs(z.n, 2 * m))
        mine.append(there.astype(float32))
    low = tree_sum(mine).astype(bfloat)
    spread = [low] + [lax.ppermute(low, "seg", pairs(planes, m)) for m in range(1, planes)]
    return tree_sum([value.astype(float32) for value in spread])


def adam_update(master, first, second, grad, factor, rate):
    clipped = grad * factor
    first_new = beta_first * first + (1.0 - beta_first) * clipped
    second_new = beta_second * second + (1.0 - beta_second) * clipped * clipped
    moment_hat = first_new / (1.0 - beta_first**STEP)
    square_hat = second_new / (1.0 - beta_second**STEP)
    master_new = master - rate * (
        moment_hat / (jnp.sqrt(square_hat) + adam_epsilon) + weight_decay * master
    )
    return (master_new, first_new, second_new)


RATES = (
    learn_rate, learn_rate, learn_rate, fast_rate, learn_rate, learn_rate, learn_rate, fast_rate,
)


def update(z, squares, first_sum, second_sum, masters, firsts, seconds):
    D, O, w, cw = z.D, z.out, z.w, z.cw

    def kernel(*refs):
        sq_ref, a_ref, b_ref = refs[:3]
        ins = refs[3:27]
        loss_o, norm_o = refs[27:29]
        outs = refs[29:]
        norm = jnp.sqrt(jnp.sum(sq_ref[0:8, :], keepdims=True))
        loss_o[...] = jnp.sum(sq_ref[8:16, :], keepdims=True)
        norm_o[...] = norm
        factor = jnp.minimum(1.0, clip_limit / (norm + 1e-06))

        def rows_of(ref, start, count):
            return ref[start : start + count, :]

        base = w
        places = {
            0: [(a_ref, 0, cw, 0)],
            1: [(a_ref, cw, w, 0)],
            2: [(a_ref, cw + w + c * w, w, c * D) for c in range(2)],
            3: [(b_ref, 0, w, 0)],
            4: [(b_ref, base + c * w, w, c * D) for c in range(z.F // D)],
            5: [(b_ref, base + z.uw, z.fw, 0)],
        }

        def step(index, here, grad):
            values = adam_update(
                ins[index][here], ins[8 + index][here], ins[16 + index][here], grad, factor, RATES[index]
            )
            for kind, value in enumerate(values):
                outs[8 * kind + index][here] = value

        for index, pieces in places.items():
            for ref, start, count, lane in pieces:
                step(index, (slice(0, count), slice(lane, lane + D)), rows_of(ref, start, count))
        start = base + z.uw + z.fw
        for g in range(D // O):
            here = (slice(g * z.hw, (g + 1) * z.hw), slice(0, O))
            step(6, here, b_ref[start : start + z.hw, g * O : (g + 1) * O])
        gains = a_ref[cw + 3 * w : cw + 3 * w + 8, :][:5, :w]
        step(7, (slice(0, 5), slice(0, w)), gains)

    vmem = pl.BlockSpec(memory_space=pltpu.VMEM)
    outs = [jax.ShapeDtypeStruct((1, 1), float32)] * 2
    outs += [jax.ShapeDtypeStruct(m.shape, float32) for m in masters] * 3
    return pl.pallas_call(
        kernel,
        out_shape=outs,
        in_specs=[vmem] * 27,
        out_specs=[vmem] * 26,
        compiler_params=pltpu.CompilerParams(vmem_limit_bytes=VMEM_LIMIT),
        name="update",
    )(squares, first_sum, second_sum, *masters, *firsts, *seconds)


def on_device(*arguments):
    feats, spectral, target, valid_samples, stem_weights = arguments[:5]
    masters, firsts, seconds = arguments[5:13], arguments[13:21], arguments[21:29]
    n = lax.axis_size("tm")
    planes = lax.axis_size("seg")
    z = Sizes(n, feats, spectral, target, masters[0], masters[4])
    S, T, D = z.segments, z.tokens, z.D
    place = lax.axis_index("tm")
    portion, member = place // S, place % S

    if z.direct:
        blob = pack_weights(z, jnp.reshape(place, (1,)).astype(jnp.int32), *masters)
        weights = (lax.all_gather(blob, "tm", axis=0),)
    else:
        weights = [lax.all_gather(a.astype(bfloat), "tm", axis=0, tiled=True) for a in masters[:7]]
        gains = lax.all_gather(masters[7].astype(bfloat), "tm", axis=1, tiled=True)
        weights.append(jnp.pad(gains.astype(float32), ((0, 3), (0, 0))))
    groups = [[p * S + i for i in range(S)] for p in range(z.parts)]
    moved = lax.all_to_all(
        pack_tokens(z, feats, spectral, target),
        "tm", 0, 0, axis_index_groups=None if z.parts == 1 else groups, tiled=True,
    ).reshape(T, -1)
    spectral_all, halo = None, None
    if z.parts > 1:
        spectral_all = lax.all_gather(
            moved[:, z.frame : z.frame + D], "tm", axis=0, tiled=True,
            axis_index_groups=[[p * S + i for p in range(z.parts)] for i in range(S)],
        )
        tail = jnp.pad(moved[T - 1 :, z.frame // 2 : z.frame], ((0, 15), (0, 0)))
        lead = jnp.pad(moved[:1, : z.frame // 2], ((0, 15), (0, 0)))
        halo = (
            lax.ppermute(tail, "tm", [(i, i + S) for i in range(n - S)]),
            lax.ppermute(lead, "tm", [(i + S, i) for i in range(n - S)]),
        )
    local_count = jnp.sum(valid_samples)[None]
    if z.direct:
        counts = [local_count] + [lax.ppermute(local_count, "seg", pairs(planes, m)) for m in range(1, planes)]
        sample_count = tree_sum(counts).astype(float32)
    else:
        sample_count = lax.psum(local_count, "seg").astype(float32)
    meta = jnp.concatenate(
        [
            jnp.stack([portion * T, lax.dynamic_index_in_dim(valid_samples, member, keepdims=False)]),
            lax.dynamic_index_in_dim(stem_weights, member, keepdims=False),
            jnp.stack([place // 2, place % 2]),
        ]
    ).astype(jnp.int32)

    stream, slope, normed, sn, q, k, v, att = front(z, moved, spectral_all, halo, weights)
    second = middle(z, meta, sample_count, stream, att, moved, moved, weights)
    do, mid, misc = second[:3]
    dq, dkv = attend_back(z, q, k, v, do)
    first = back(z, meta, moved, spectral_all, halo, stream, slope, normed, sn, mid, dq, dkv, misc, weights)

    if z.direct:
        second_sum = reduce_blocks(z, second[3], second[4], planes)
        first_sum = reduce_blocks(z, first[0], first[1], planes)
        loss_row = z.first_rows - 16 + 5
        real = (iota(first_sum.shape, 0) != loss_row).astype(float32)
        masked = first_sum * real
        squares = jnp.sum((masked * masked).reshape(-1, 8, D), 0) + jnp.sum(
            (second_sum * second_sum).reshape(-1, 8, D), 0
        )
        squares = squares[:, :LANES] + squares[:, LANES : 2 * LANES] + squares[:, 2 * LANES :]
        loss = jnp.pad(first_sum[loss_row : loss_row + 1, :LANES] * (1.0 / n), ((0, 7), (0, 0)))
        both = jnp.concatenate([squares, loss], 0)
        both = both + lax.ppermute(both, "tm", pairs(n, 1))
        both = tree_sum([both] + [lax.ppermute(both, "tm", pairs(n, 2 * m)) for m in range(1, n // 2)])
        result = update(z, both, first_sum, second_sum, masters, firsts, seconds)
        return (result[0].reshape(()), sample_count.reshape(()), result[1].reshape(()), *result[2:])

    grads = (first[0], first[1], first[2], second[3], second[4], second[5], second[6])
    shards = [lax.psum_scatter(g, "tm", scatter_dimension=0, tiled=True) for g in grads]
    shards.append(lax.psum_scatter(first[3][:5], "tm", scatter_dimension=1, tiled=True))
    reduced = lax.psum(tuple(shards), "seg")
    loss_sum = lax.psum(jnp.sum(first[3][5]), ("seg", "tm"))
    squares = lax.psum(sum(jnp.sum(shard * shard) for shard in reduced), "tm")
    grad_norm = jnp.sqrt(squares)
    factor = jnp.minimum(1.0, clip_limit / (grad_norm + 1e-06))
    updated = [
        adam_update(m, f, s, g, factor, r)
        for m, f, s, g, r in zip(masters, firsts, seconds, reduced, RATES)
    ]
    return (
        loss_sum, sample_count.reshape(()), grad_norm,
        *[u[0] for u in updated], *[u[1] for u in updated], *[u[2] for u in updated],
    )


def solution(mesh):
    rows, columns = P("tm", None), P(None, "tm")
    leaves = (rows,) * 7 + (columns,)
    tokens = P("seg", "tm", None)
    return jax.shard_map(
        on_device,
        mesh=mesh,
        in_specs=(tokens, tokens, tokens, P("seg"), P("seg", None)) + leaves * 3,
        out_specs=(P(), P(), P()) + leaves * 3,
        check_vma=False,
    )
```

time: 1010 us -> 273 us (0.27)
  waiting for transfers between devices: 484 us -> 85.4 us
  matrix products: 152 us -> 0 us
  local copies, waits for them, and re-layouts: 142 us -> 4.77 us
  blocking collectives: 131 us -> 0 us
  Pallas kernels: 0 us -> 115 us
  other arithmetic: 65.4 us -> 5.24 us
  starting transfers between devices: 5.83 us -> 43.9 us
    reduce_scatter x8 -> x0, waiting for transfers between devices: 403 us -> none  [the longest x1 123 us: on_device(): lax.psum_scatter(keyval_grad_all, 'tm', scatter_dimension=1, tiled=True)]
    dot_general x56 -> x0, matrix products: 152 us -> none  [the longest x7 27.2 us: outer_sum(): lax.dot_general(left, right, (((0,), (0,)), ((), ())), preferred_element_...]
    pallas_call x0 -> x7, Pallas kernels: none -> 115 us  [the longest x1 37.9 us: front(): pl.pallas_call(kernel, grid=(1,), out_shape=[jax.ShapeDtypeStruct(s, d) f...]
    psum x3 -> x0, blocking collectives: 73.4 us -> none  [the longest x1 39.5 us: on_device(): loss_sum, sample_count = lax.psum((loss_part, count_part), ('seg', 'tm'))]
    all_gather x5 -> x0, blocking collectives: 57.9 us -> none  [the longest x1 15.9 us: on_device(): lax.all_gather(out_weight.astype(bfloat), 'tm', axis=0, tiled=True)]
    dynamic_update_slice x8 -> x0, local copies, waits for them, and re-layouts: 50.2 us -> none  [grad_step(): lax.dynamic_update_slice_in_dim(keyval_grad, joined, position * block_siz...]
    ppermute x2 -> x21, waiting for transfers between devices: 0.01 us -> 47 us  [the longest x6 21.3 us: reduce_blocks(): lax.ppermute(low, 'seg', pairs(planes, m))]
    slice x20 -> x0, local copies, waits for them, and re-layouts: 43.9 us -> none  [the longest x8 19.5 us: split_block(): block[..., :half_width]]
  transfers between devices with their start and end apart: 16 -> 23, of which waited for: 11 -> 16; matrix products, arithmetic and copies ran while one was open for 15% -> 3% of each run, Pallas kernels for 0% -> 2%
where the time goes in v1:
time: 273 us; the launch traced here: 272 us
  Pallas kernels  115 us (42%)
  waiting for transfers between devices  85.4 us (31%)
  starting transfers between devices  43.9 us (16%)
  between operations  18 us (7%)
  other arithmetic  5.24 us (2%)
  local copies, waits for them, and re-layouts  4.77 us (2%)
    pallas_call x1, Pallas kernels, front(): pl.pallas_call(kernel, grid=(1,), out_shape=[jax.ShapeDtypeStruct(s, d) f...  37.9 us
    all_to_all x1, waiting for transfers between devices, on_device(): lax.all_to_all(pack_tokens(z, feats, spectral, target), 'tm', 0, 0, axis_...  34.7 us
    pallas_call x1, Pallas kernels, middle(): pl.pallas_call(kernel, grid=(1,), out_shape=[jax.ShapeDtypeStruct(s, d) f...  25.9 us
    ppermute x6, starting transfers between devices, reduce_blocks(): lax.ppermute(low, 'seg', pairs(planes, m))  23 us
    ppermute x6, waiting for transfers between devices, reduce_blocks(): lax.ppermute(low, 'seg', pairs(planes, m))  21.3 us
    pallas_call x1, Pallas kernels, attend_back(): pl.pallas_call(kernel, grid=(H,), out_shape=[jax.ShapeDtypeStruct((T, W),...  21.1 us
    ppermute x6, waiting for transfers between devices, reduce_blocks(): there = lax.ppermute(blocks[m].astype(bfloat), 'tm', pairs(z.n, 2 * m))  18.6 us
    pallas_call x1, Pallas kernels, back(): pl.pallas_call(kernel, grid=(1,), out_shape=[jax.ShapeDtypeStruct(s, d) f...  16.2 us
  transfers between devices with their start and end apart: 23, of which 16 were waited for; matrix products, arithmetic and copies ran while one was open for 3% of the time, Pallas kernels for 2%

profile of v1, /device:TPU:0, one launch (start us, length us, event | category | flops | bytes accessed | tf_op | source)
XLA Modules:
  0.0 272.1 jit_solution(15147546503625704657)
XLA Ops:
  7.2 0.0 copy-start
  7.2 0.0 all-gather.3.cloned.1.call-start
  7.3 2.4 pack_weights.1
  9.7 0.0 all-gather.3.cloned.1.call-update
  9.7 2.5 copy.56.f_ref
  12.2 6.5 %pack_tokens.1 = bf16[8,128,1280]{2,1,0:T(8,128)(2,1)} custom-call(bf16[8,512,192]{2,1,0:T(8,128)(2,1)} %copy.56.f_ref, bf16[8,128,384]{2,1,0:T(8,128)(2,1)} %s_ref.1, bf16[8,128,128]{2,1,0:T(8,128)(2,1)} %t_ref.1), custom_call_target="tpu_custom_call" | custom-call | tf_op jit(solution)/shard_map/pack_tokens/pallas_call | solution.py:168
  18.7 5.3 %all-to-all-start = ((bf16[8,128,1280]{2,1,0:T(8,128)(2,1)}), bf16[8,128,1280]{2,1,0:T(8,128)(2,1)S(1)}, u32[]{:S(2)}, u32[]{:S(2)}) async-start(bf16[8,128,1280]{2,1,0:T(8,128)(2,1)} %pack_tokens.1), calls=%async_computation | async-start | bytes 5242880 | tf_op jit(solution)/shard_map/all_to_all | solution.py:832
  24.0 0.6 reduce_sum.27
  24.7 3.6 %collective-permute-start.2 = (s32[1]{0:T(128)}, s32[1]{0:T(128)}, u32[]{:S(2)}, u32[]{:S(2)}) collective-permute-start(s32[1]{0:T(128)} %bitcast.6), channel_id=1, source_target_pairs={{0,24},{8,16},{16,8},{24,0},{1,25},{9,17},{17,9},{25,1},{2,26},{10... | collective-permute-start | bytes 20 | tf_op jit(solution)/shard_map/ppermute | solution.py:850
  28.3 0.0 collective-permute-start.1
  28.3 0.8 collective-permute-start
  29.1 0.6 dynamic_slice.8
  29.6 0.2 dynamic-slice_reduce_fusion
  29.8 1.2 concatenate.6.meta_ref
  31.1 0.8 collective-permute-done
  33.2 0.0 collective-permute-done.2
  34.5 34.7 %all-to-all-done = bf16[8,128,1280]{2,1,0:T(8,128)(2,1)S(1)} async-done(((bf16[8,128,1280]{2,1,0:T(8,128)(2,1)}), bf16[8,128,1280]{2,1,0:T(8,128)(2,1)S(1)}, u32[]{:S(2)}, u32[]{:S(2)}) %all-to-all-start) | async-done | bytes 2621472 | tf_op jit(solution)/shard_map/all_to_all | solution.py:832
  69.2 3.7 %all-gather.3.cloned.1.call-done = bf16[6400,384]{1,0:T(8,128)(2,1)} async-done(((bf16[800,384]{1,0:T(8,128)(2,1)}), bf16[6400,384]{1,0:T(8,128)(2,1)}) %all-gather.3.cloned.1.call-update) | async-done | bytes 4915216 | tf_op jit(solution)/shard_map/all_gather | solution.py:826
  72.9 37.9 %front.1 = (f32[1024,384]{1,0:T(8,128)}, f32[1024,384]{1,0:T(8,128)}, bf16[1024,384]{1,0:T(8,128)(2,1)}, bf16[1024,384]{1,0:T(8,128)(2,1)}, bf16[1024,1024]{1,0:...) custom-call(bf16[1024,1280]{1,0:T(8,128)(2,1)} %bitcast.42, ...), custom_call_target="tpu_custom_call" | custom-call | flops 30000001024 | bytes 20000000 | tf_op jit(solution)/shard_map/front/pallas_call | solution.py:319
  110.8 25.9 %middle.1 = (bf16[1024,1024]{1,0:T(8,128)(2,1)}, f32[1024,384]{1,0:T(8,128)}, f32[8,384]{1,0:T(8,128)}, f32[4,448,384]{2,1,0:T(8,128)}, bf16[4,448,384]{2,1,0:T(8,128)(2,1)}) custom-call(s32[8]{0:T(128)} %concatenate.6.meta_ref, f32[1]{0:T(128)} %convert_element_type.84.count_ref, f32[1024,384]{1,0:T(8,128)} %get-tuple-element.70.stream_ref, ...), custom_call_target="tpu_custom_call" | custom-call | flops 15000000512 | bytes 20000000 | tf_op jit(solution)/shard_map/middle/pallas_call | solution.py:517
  136.7 21.1 %attend_back.1 = (bf16[1024,1024]{1,0:T(8,128)(2,1)}, bf16[2,384,1024]{2,1,0:T(8,128)(2,1)}) custom-call(bf16[1024,1024]{1,0:T(8,128)(2,1)} %get-tuple-element.76.q_ref, bf16[1024,1024]{1,0:T(8,128)(2,1)} %get-tuple-element.77.k_ref, bf16[1024,1024]{1,0:T(8,128)(2,1)} %get-tuple-element.78.v_ref, bf16[1024,1024]{1,0:T(8,128)(2,1)} %get-tuple-element.79.do_ref), custom_call_target="tpu_custom_call" | custom-call | flops 40000000000 | bytes 12000000 | tf_op jit(solution)/shard_map/attend_back/pallas_call | solution.py:554
  157.7 16.2 %back.1 = (f32[4,352,384]{2,1,0:T(8,128)}, bf16[4,352,384]{2,1,0:T(8,128)(2,1)}) custom-call(s32[8]{0:T(128)} %concatenate.6.meta_ref, bf16[1024,1280]{1,0:T(8,128)(2,1)} %bitcast.45, bf16[1024,1280]{1,0:T(8,128)(2,1)} %bitcast.46, f32[1024,384]{1,0:T(8,128)} %get-tuple-element.70.stream_ref, f32[1024,384]{1,0:T(8,128)} %get-tuple-element.71.slope_ref, ...), custom_call_target="tpu_custom_call" | custom-call | flops 12000000000 | bytes 20000000 | tf_op jit(solution)/shard_map/back/pallas_call | solution.py:707
  174.0 0.3 collective-permute-start.3
  174.3 0.3 collective-permute-start.10
  174.5 2.4 collective-permute-done.3
  176.9 2.1 fusion.8
  179.0 0.1 slice_bitcast_fusion.7
  179.1 1.5 collective-permute-start.4
  180.7 1.0 collective-permute-start.6
  181.7 1.0 collective-permute-start.5
  182.7 0.0 collective-permute-done.10
  182.7 0.3 fusion.7
  183.0 0.1 slice_bitcast_fusion.4
  183.2 1.5 collective-permute-start.11
  184.7 1.0 collective-permute-start.13
  185.7 2.8 %collective-permute-done.4 = bf16[352,384]{1,0:T(8,128)(2,1)S(1)} collective-permute-done((bf16[352,384]{1,0:T(8,128)(2,1)S(1)}, bf16[352,384]{1,0:T(8,128)(2,1)S(1)}, u32[]{:S(2)}, u32[]{:S(2)}) %collective-permute-start.4) | collective-permute-done | bytes 270368 | tf_op jit(solution)/shard_map/ppermute | solution.py:734
  188.5 1.0 collective-permute-start.12
  189.5 5.3 %collective-permute-done.6 = bf16[352,384]{1,0:T(8,128)(2,1)S(1)} collective-permute-done((bf16[352,384]{1,0:T(8,128)(2,1)S(1)}, bf16[352,384]{1,0:T(8,128)(2,1)S(1)}, u32[]{:S(2)}, u32[]{:S(2)}) %collective-permute-start.6) | collective-permute-done | bytes 270368 | tf_op jit(solution)/shard_map/ppermute | solution.py:734
  194.8 2.1 collective-permute-done.5
  196.8 0.1 fusion.5
  197.0 3.4 %collective-permute-start.9 = (bf16[352,384]{1,0:T(8,128)(2,1)S(1)}, bf16[352,384]{1,0:T(8,128)(2,1)S(1)}, u32[]{:S(2)}, u32[]{:S(2)}) collective-permute-start(bf16[352,384]{1,0:T(8,128)(2,1)S(1)} %fusion.5), channel_id=1, source_target_pairs={{0,24},{8,16},{16,8},{24,0},{1,25},{9,17},{17,9},{25,1},{2,26},{10... | collective-permute-start | bytes 811016 | tf_op jit(solution)/shard_map/ppermute | solution.py:737
  200.4 1.3 collective-permute-done.11
  201.7 1.5 collective-permute-start.7
  203.2 5.7 %collective-permute-done.13 = bf16[448,384]{1,0:T(8,128)(2,1)S(1)} collective-permute-done((bf16[448,384]{1,0:T(8,128)(2,1)S(1)}, bf16[448,384]{1,0:T(8,128)(2,1)S(1)}, u32[]{:S(2)}, u32[]{:S(2)}) %collective-permute-start.13) | collective-permute-done | bytes 344096 | tf_op jit(solution)/shard_map/ppermute | solution.py:734
  208.9 1.3 collective-permute-done.12
  210.3 0.2 fusion.2
  210.4 3.4 %collective-permute-start.16 = (bf16[448,384]{1,0:T(8,128)(2,1)S(1)}, bf16[448,384]{1,0:T(8,128)(2,1)S(1)}, u32[]{:S(2)}, u32[]{:S(2)}) collective-permute-start(bf16[448,384]{1,0:T(8,128)(2,1)S(1)} %fusion.2), channel_id=1, source_target_pairs={{0,24},{8,16},{16,8},{24,0},{1,25},{9,17},{17,9},{25,1},{2,26},{10... | collective-permute-start | bytes 1032200 | tf_op jit(solution)/shard_map/ppermute | solution.py:737
  213.8 14.7 %collective-permute-start.14 = (bf16[448,384]{1,0:T(8,128)(2,1)S(1)}, bf16[448,384]{1,0:T(8,128)(2,1)S(1)}, u32[]{:S(2)}, u32[]{:S(2)}) collective-permute-start(bf16[448,384]{1,0:T(8,128)(2,1)S(1)} %fusion.2), channel_id=1, source_target_pairs={{0,8},{8,0},{16,24},{24,16},{1,9},{9,1},{17,25},{25,17},{2,10},{10... | collective-permute-start | bytes 1032200 | tf_op jit(solution)/shard_map/ppermute | solution.py:737
  228.6 7.8 %collective-permute-done.8 = bf16[352,384]{1,0:T(8,128)(2,1)S(1)} collective-permute-done((bf16[352,384]{1,0:T(8,128)(2,1)S(1)}, bf16[352,384]{1,0:T(8,128)(2,1)S(1)}, u32[]{:S(2)}, u32[]{:S(2)}) %collective-permute-start.8) | collective-permute-done | bytes 270368 | tf_op jit(solution)/shard_map/ppermute | solution.py:737
  236.4 0.0 collective-permute-done.7
  236.4 0.2 bitcast_reduce_fusion.1
  236.6 0.0 collective-permute-done.16
  236.6 13.5 %collective-permute-done.15 = bf16[448,384]{1,0:T(8,128)(2,1)S(1)} collective-permute-done((bf16[448,384]{1,0:T(8,128)(2,1)S(1)}, bf16[448,384]{1,0:T(8,128)(2,1)S(1)}, u32[]{:S(2)}, u32[]{:S(2)}) %collective-permute-start.15) | collective-permute-done | bytes 344096 | tf_op jit(solution)/shard_map/ppermute | solution.py:737
  250.1 1.1 bitcast_reduce_fusion
  251.2 0.1 collective-permute-start.17
  251.3 1.2 collective-permute-done.17
  252.4 2.1 collective-permute-start.20
  254.5 0.5 collective-permute-start.19
  255.0 0.9 collective-permute-start.18
  255.9 1.1 collective-permute-done.20
  257.0 1.2 collective-permute-done.19
  258.1 0.5 collective-permute-done.18
  258.6 0.6 add_add_fusion.2.refs_0_
  259.2 4.9 %update.1 = (f32[1,1]{1,0:T(1,128)}, f32[1,1]{1,0:T(1,128)}, f32[192,384]{1,0:T(8,128)}, f32[48,384]{1,0:T(8,128)}, f32[48,768]{1,0:T(8,128)}, /*index=5*/f32[48...) custom-call(f32[16,128]{1,0:T(8,128)} %add_add_fusion.2.refs_0_, ...), custom_call_target="tpu_custom_call" | custom-call | tf_op jit(solution)/shard_map/update/pallas_call | solution.py:804
  (26 shorter events, 0.1 us)
Async XLA Ops:
  7.2 22.4 %copy-start = (s32[8,4]{0,1:T(4,128)S(1)}, s32[8,4]{0,1:T(4,128)}, u32[]{:S(2)}) copy-start(s32[8,4]{0,1:T(4,128)} %param.33) | copy-start | bytes 388
  7.2 2.5 copy-start.5
  7.2 65.6 %all-gather.3.cloned.1.call-start = ((), (), s32[]{:S(2)}) async-start(), calls=%async_computation.1 | async-start | bytes 5529600 | tf_op jit(solution)/shard_map/all_gather | solution.py:826
  18.7 5.3 %copy-start.7 = (s32[8]{0:T(128)S(1)}, s32[8]{0:T(128)}, u32[]{:S(2)}) copy-start(s32[8]{0:T(128)} %param.32) | copy-start | bytes 100
  18.7 50.5 %all-to-all-start = ((bf16[8,128,1280]{2,1,0:T(8,128)(2,1)}), bf16[8,128,1280]{2,1,0:T(8,128)(2,1)S(1)}, u32[]{:S(2)}, u32[]{:S(2)}) async-start(bf16[8,128,1280]{2,1,0:T(8,128)(2,1)} %pack_tokens.1), calls=%async_computation | async-start | bytes 5242880 | tf_op jit(solution)/shard_map/all_to_all | solution.py:832
  24.7 8.6 %collective-permute-start.2 = (s32[1]{0:T(128)}, s32[1]{0:T(128)}, u32[]{:S(2)}, u32[]{:S(2)}) collective-permute-start(s32[1]{0:T(128)} %bitcast.6), channel_id=1, source_target_pairs={{0,24},{8,16},{16,8},{24,0},{1,25},{9,17},{17,9},{25,1},{2,26},{10... | collective-permute-start | bytes 20 | tf_op jit(solution)/shard_map/ppermute | solution.py:850
  28.3 5.0 %collective-permute-start.1 = (s32[1]{0:T(128)}, s32[1]{0:T(128)}, u32[]{:S(2)}, u32[]{:S(2)}) collective-permute-start(s32[1]{0:T(128)} %bitcast.6), channel_id=1, source_target_pairs={{0,16},{8,24},{16,0},{24,8},{1,17},{9,25},{17,1},{25,9},{2,18},{10... | collective-permute-start | bytes 20 | tf_op jit(solution)/shard_map/ppermute | solution.py:850
  28.3 3.6 %collective-permute-start = (s32[1]{0:T(128)}, s32[1]{0:T(128)}, u32[]{:S(2)}, u32[]{:S(2)}) collective-permute-start(s32[1]{0:T(128)} %bitcast.6), channel_id=1, source_target_pairs={{0,8},{8,0},{16,24},{24,16},{1,9},{9,1},{17,25},{25,17},{2,10},{10... | collective-permute-start | bytes 20 | tf_op jit(solution)/shard_map/ppermute | solution.py:850
  69.2 3.7 %copy-start.3 = (bf16[8,128,1280]{2,1,0:T(8,128)(2,1)}, bf16[8,128,1280]{2,1,0:T(8,128)(2,1)S(1)}, u32[]{:S(2)}) copy-start(bf16[8,128,1280]{2,1,0:T(8,128)(2,1)S(1)} %all-to-all-done) | copy-start | bytes 7864324
  157.7 16.6 %copy-start.6 = (bf16[4,448,384]{2,1,0:T(8,128)(2,1)S(1)}, bf16[4,448,384]{2,1,0:T(8,128)(2,1)}, u32[]{:S(2)}) copy-start(bf16[4,448,384]{2,1,0:T(8,128)(2,1)} %get-tuple-element.86) | copy-start | bytes 4128772
  174.0 3.0 %collective-permute-start.3 = (bf16[4,352,384]{2,1,0:T(8,128)(2,1)}, bf16[4,352,384]{2,1,0:T(8,128)(2,1)S(1)}, u32[]{:S(2)}, u32[]{:S(2)}) collective-permute-start(bf16[4,352,384]{2,1,0:T(8,128)(2,1)} %get-tuple-element.84), channel_id=1, source_target_pairs={{0,1},{1,0},{2,3},{3,2},{4,5},{5,4},{6,7},{7,6},{8,9},{9,8},{10,11... | collective-permute-start | bytes 3244040 | tf_op jit(solution)/shard_map/ppermute | solution.py:731
  174.3 8.4 %collective-permute-start.10 = (bf16[4,448,384]{2,1,0:T(8,128)(2,1)S(1)}, bf16[4,448,384]{2,1,0:T(8,128)(2,1)S(1)}, u32[]{:S(2)}, u32[]{:S(2)}) collective-permute-start(bf16[4,448,384]{2,1,0:T(8,128)(2,1)S(1)} %copy-done.6), channel_id=1, source_target_pairs={{0,1},{1,0},{2,3},{3,2},{4,5},{5,4},{6,7},{7,6},{8,9},{9,8},{10,11... | collective-permute-start | bytes 4128776 | tf_op jit(solution)/shard_map/ppermute | solution.py:731
  176.9 5.7 %copy-start.2 = (f32[4,448,384]{2,1,0:T(8,128)S(1)}, f32[4,448,384]{2,1,0:T(8,128)}, u32[]{:S(2)}) copy-start(f32[4,448,384]{2,1,0:T(8,128)} %get-tuple-element.85) | copy-start | bytes 8257540
  179.1 9.4 %collective-permute-start.4 = (bf16[352,384]{1,0:T(8,128)(2,1)S(1)}, bf16[352,384]{1,0:T(8,128)(2,1)S(1)}, u32[]{:S(2)}, u32[]{:S(2)}) collective-permute-start(bf16[352,384]{1,0:T(8,128)(2,1)S(1)} %get-tuple-element.124), channel_id=1, source_target_pairs={{0,2},{1,3},{2,0},{3,1},{4,6},{5,7},{6,4},{7,5},{8,10},{9,11},{10,... | collective-permute-start | bytes 811016 | tf_op jit(solution)/shard_map/ppermute | solution.py:734
  180.7 14.1 %collective-permute-start.6 = (bf16[352,384]{1,0:T(8,128)(2,1)S(1)}, bf16[352,384]{1,0:T(8,128)(2,1)S(1)}, u32[]{:S(2)}, u32[]{:S(2)}) collective-permute-start(bf16[352,384]{1,0:T(8,128)(2,1)S(1)} %get-tuple-element.125), channel_id=1, source_target_pairs={{0,6},{1,7},{2,4},{3,5},{4,2},{5,3},{6,0},{7,1},{8,14},{9,15},{10,... | collective-permute-start | bytes 811016 | tf_op jit(solution)/shard_map/ppermute | solution.py:734
  181.7 15.2 %collective-permute-start.5 = (bf16[352,384]{1,0:T(8,128)(2,1)S(1)}, bf16[352,384]{1,0:T(8,128)(2,1)S(1)}, u32[]{:S(2)}, u32[]{:S(2)}) collective-permute-start(bf16[352,384]{1,0:T(8,128)(2,1)S(1)} %get-tuple-element.126), channel_id=1, source_target_pairs={{0,4},{1,5},{2,6},{3,7},{4,0},{5,1},{6,2},{7,3},{8,12},{9,13},{10,... | collective-permute-start | bytes 811016 | tf_op jit(solution)/shard_map/ppermute | solution.py:734
  183.2 18.6 %collective-permute-start.11 = (bf16[448,384]{1,0:T(8,128)(2,1)S(1)}, bf16[448,384]{1,0:T(8,128)(2,1)S(1)}, u32[]{:S(2)}, u32[]{:S(2)}) collective-permute-start(bf16[448,384]{1,0:T(8,128)(2,1)S(1)} %get-tuple-element.121), channel_id=1, source_target_pairs={{0,2},{1,3},{2,0},{3,1},{4,6},{5,7},{6,4},{7,5},{8,10},{9,11},{10,... | collective-permute-start | bytes 1032200 | tf_op jit(solution)/shard_map/ppermute | solution.py:734
  184.7 24.3 %collective-permute-start.13 = (bf16[448,384]{1,0:T(8,128)(2,1)S(1)}, bf16[448,384]{1,0:T(8,128)(2,1)S(1)}, u32[]{:S(2)}, u32[]{:S(2)}) collective-permute-start(bf16[448,384]{1,0:T(8,128)(2,1)S(1)} %get-tuple-element.122), channel_id=1, source_target_pairs={{0,6},{1,7},{2,4},{3,5},{4,2},{5,3},{6,0},{7,1},{8,14},{9,15},{10,... | collective-permute-start | bytes 1032200 | tf_op jit(solution)/shard_map/ppermute | solution.py:734
  188.5 21.7 %collective-permute-start.12 = (bf16[448,384]{1,0:T(8,128)(2,1)S(1)}, bf16[448,384]{1,0:T(8,128)(2,1)S(1)}, u32[]{:S(2)}, u32[]{:S(2)}) collective-permute-start(bf16[448,384]{1,0:T(8,128)(2,1)S(1)} %get-tuple-element.123), channel_id=1, source_target_pairs={{0,4},{1,5},{2,6},{3,7},{4,0},{5,1},{6,2},{7,3},{8,12},{9,13},{10,... | collective-permute-start | bytes 1032200 | tf_op jit(solution)/shard_map/ppermute | solution.py:734
  197.0 16.9 %collective-permute-start.9 = (bf16[352,384]{1,0:T(8,128)(2,1)S(1)}, bf16[352,384]{1,0:T(8,128)(2,1)S(1)}, u32[]{:S(2)}, u32[]{:S(2)}) collective-permute-start(bf16[352,384]{1,0:T(8,128)(2,1)S(1)} %fusion.5), channel_id=1, source_target_pairs={{0,24},{8,16},{16,8},{24,0},{1,25},{9,17},{17,9},{25,1},{2,26},{10... | collective-permute-start | bytes 811016 | tf_op jit(solution)/shard_map/ppermute | solution.py:737
  200.4 36.0 %collective-permute-start.8 = (bf16[352,384]{1,0:T(8,128)(2,1)S(1)}, bf16[352,384]{1,0:T(8,128)(2,1)S(1)}, u32[]{:S(2)}, u32[]{:S(2)}) collective-permute-start(bf16[352,384]{1,0:T(8,128)(2,1)S(1)} %fusion.5), channel_id=1, source_target_pairs={{0,16},{8,24},{16,0},{24,8},{1,17},{9,25},{17,1},{25,9},{2,18},{10... | collective-permute-start | bytes 811016 | tf_op jit(solution)/shard_map/ppermute | solution.py:737
  201.7 34.7 %collective-permute-start.7 = (bf16[352,384]{1,0:T(8,128)(2,1)S(1)}, bf16[352,384]{1,0:T(8,128)(2,1)S(1)}, u32[]{:S(2)}, u32[]{:S(2)}) collective-permute-start(bf16[352,384]{1,0:T(8,128)(2,1)S(1)} %fusion.5), channel_id=1, source_target_pairs={{0,8},{8,0},{16,24},{24,16},{1,9},{9,1},{17,25},{25,17},{2,10},{10... | collective-permute-start | bytes 811016 | tf_op jit(solution)/shard_map/ppermute | solution.py:737
  210.4 26.2 %collective-permute-start.16 = (bf16[448,384]{1,0:T(8,128)(2,1)S(1)}, bf16[448,384]{1,0:T(8,128)(2,1)S(1)}, u32[]{:S(2)}, u32[]{:S(2)}) collective-permute-start(bf16[448,384]{1,0:T(8,128)(2,1)S(1)} %fusion.2), channel_id=1, source_target_pairs={{0,24},{8,16},{16,8},{24,0},{1,25},{9,17},{17,9},{25,1},{2,26},{10... | collective-permute-start | bytes 1032200 | tf_op jit(solution)/shard_map/ppermute | solution.py:737
  213.8 36.3 %collective-permute-start.15 = (bf16[448,384]{1,0:T(8,128)(2,1)S(1)}, bf16[448,384]{1,0:T(8,128)(2,1)S(1)}, u32[]{:S(2)}, u32[]{:S(2)}) collective-permute-start(bf16[448,384]{1,0:T(8,128)(2,1)S(1)} %fusion.2), channel_id=1, source_target_pairs={{0,16},{8,24},{16,0},{24,8},{1,17},{9,25},{17,1},{25,9},{2,18},{10... | collective-permute-start | bytes 1032200 | tf_op jit(solution)/shard_map/ppermute | solution.py:737
  213.8 36.3 %collective-permute-start.14 = (bf16[448,384]{1,0:T(8,128)(2,1)S(1)}, bf16[448,384]{1,0:T(8,128)(2,1)S(1)}, u32[]{:S(2)}, u32[]{:S(2)}) collective-permute-start(bf16[448,384]{1,0:T(8,128)(2,1)S(1)} %fusion.2), channel_id=1, source_target_pairs={{0,8},{8,0},{16,24},{24,16},{1,9},{9,1},{17,25},{25,17},{2,10},{10... | collective-permute-start | bytes 1032200 | tf_op jit(solution)/shard_map/ppermute | solution.py:737
  236.6 22.7 %copy-start.4 = (f32[352,384]{1,0:T(8,128)}, f32[352,384]{1,0:T(8,128)S(1)}, u32[]{:S(2)}) copy-start(f32[352,384]{1,0:T(8,128)S(1)} %get-tuple-element.118.refs_1_) | copy-start | bytes 1622020
  251.2 1.2 collective-permute-start.17
  252.4 4.5 %collective-permute-start.20 = (f32[16,128]{1,0:T(8,128)S(1)}, f32[16,128]{1,0:T(8,128)S(1)}, u32[]{:S(2)}, u32[]{:S(2)}) collective-permute-start(f32[16,128]{1,0:T(8,128)S(1)} %fusion.6), channel_id=1, source_target_pairs={{0,6},{1,7},{2,4},{3,5},{4,2},{5,3},{6,0},{7,1},{8,14},{9,15},{10,... | collective-permute-start | bytes 24584 | tf_op jit(solution)/shard_map/ppermute | solution.py:881
  254.5 3.7 %collective-permute-start.19 = (f32[16,128]{1,0:T(8,128)S(1)}, f32[16,128]{1,0:T(8,128)S(1)}, u32[]{:S(2)}, u32[]{:S(2)}) collective-permute-start(f32[16,128]{1,0:T(8,128)S(1)} %fusion.6), channel_id=1, source_target_pairs={{0,4},{1,5},{2,6},{3,7},{4,0},{5,1},{6,2},{7,3},{8,12},{9,13},{10,... | collective-permute-start | bytes 24584 | tf_op jit(solution)/shard_map/ppermute | solution.py:881
  255.0 3.7 %collective-permute-start.18 = (f32[16,128]{1,0:T(8,128)S(1)}, f32[16,128]{1,0:T(8,128)S(1)}, u32[]{:S(2)}, u32[]{:S(2)}) collective-permute-start(f32[16,128]{1,0:T(8,128)S(1)} %fusion.6), channel_id=1, source_target_pairs={{0,2},{1,3},{2,0},{3,1},{4,6},{5,7},{6,4},{7,5},{8,10},{9,11},{10,... | collective-permute-start | bytes 24584 | tf_op jit(solution)/shard_map/ppermute | solution.py:881
  259.2 4.9 %copy-start.1 = (s32[8,4]{0,1:T(4,128)S(1)}, s32[8,4]{0,1:T(4,128)}, u32[]{:S(2)}) copy-start(s32[8,4]{0,1:T(4,128)} %param.33) | copy-start | bytes 388
Sparse Core Ops, SparseCore 0:
  9.9 62.8 all-gather.2
